TPU v7x, 512 devices: a whole 4x8x8 slice. The times are simulated.
512 devices in a mesh: gx: 32 (over x_lo, z, core), gy: 16 (over x_hi, y).
Axes of the slice: x: 4 (x_hi: 2, x_lo: 2; x = x_hi * 2 + x_lo), y: 8, z: 8, core: 2. Of those that a mesh axis runs over, the one named last changes fastest.
Arguments:
- noise: float32 [512, 1024, 512], P('gx', 'gy'), may hold values from -6 to 6
- rate: float32 [512, 1024], P('gx', 'gy'), may hold values from -0.3 to 0.3
- coupling: float32 [512, 1024], P('gx', 'gy'), may hold values from 0.05 to 0.2
- vertical: float32 [64, 64], replicated, may hold values from -0.12 to 0.12
- coeffs: float32 [4], replicated, may hold values from 0.3 to 1
- columns: int32 [512, 64], P(('gx', 'gy')), may hold values from 0 to 1023
- slots: int32 [512, 64], P(('gx', 'gy')), may hold values from 0 to 63, each once within a row
Outputs:
- sample: float32 [512, 1024, 512], P('gx', 'gy')
- grad_blocks: float32 [32768, 1024], P(('gx', 'gy'))
Inputs may be any that keep to these rules, and one draw needn't show every extreme that they name: Each row of slots is a permutation; slot k is owned by the device at gx index k // 2 in the same gy column.
All inputs are finite; a program needn't handle non-finite values.
Results may differ from a plain program's by a relative error of at most 0.0002.
Values sent between devices are 32-bit elements; how exact they have to be, the bound alone decides.
A program may use at most 64 MiB of HBM per device.

v0:
```python
import jax
import jax.numpy as jnp
from jax import lax
from jax.sharding import PartitionSpec as P


def with_halo(cells, sides, width):
    for axis, dim in sides:
        count = lax.axis_size(axis)
        ends = count - 1
        head = lax.slice_in_dim(cells, 0, width, axis=dim)
        tail = lax.slice_in_dim(cells, cells.shape[dim] - width, cells.shape[dim], axis=dim)
        cells = jnp.concatenate(
            [
                lax.ppermute(tail, axis, [(i, (i + 1) % count) for i in range(ends)]),
                cells,
                lax.ppermute(head, axis, [((i + 1) % count, i) for i in range(ends)]),
            ],
            axis=dim,
        )
    return cells


def operate(extended, coef, vertical):
    core = extended[1:-1, 1:-1]
    beside = extended[2:, 1:-1] + extended[:-2, 1:-1] + extended[1:-1, 2:] + extended[1:-1, :-2]
    column = jnp.dot(
        core.reshape(-1, vertical.shape[0]),
        vertical.T,
        precision=lax.Precision.HIGHEST,
        preferred_element_type=jnp.float32,
    ).reshape(core.shape)
    return coef[:, :, 0:1] * core + column - coef[:, :, 1:2] * beside


def widen(field):
    return with_halo(field, (("gx", 0), ("gy", 1)), 1)


def shards(noise, rate, coupling, vertical, coeffs, columns, slots):
    coef = jnp.stack([rate, coupling], axis=-1)
    first = operate(widen(noise), coef, vertical)
    second = 2.0 * operate(widen(first), coef, vertical) - noise
    third = 2.0 * operate(widen(second), coef, vertical) - first
    sample = coeffs[0] * noise + coeffs[1] * first + coeffs[2] * second + coeffs[3] * third
    extended = widen(sample)
    tile_y = noise.shape[1]
    span_y = tile_y + 2
    width_all = noise.shape[2]
    flat_field = extended.reshape(-1, width_all)
    places = columns[0]
    cell_x = places // tile_y + 1
    cell_y = places % tile_y + 1
    center = flat_field[cell_x * span_y + cell_y]
    slope_x = (
        flat_field[(cell_x + 1) * span_y + cell_y] - flat_field[(cell_x - 1) * span_y + cell_y]
    ) * 0.5
    slope_y = (
        flat_field[cell_x * span_y + cell_y + 1] - flat_field[cell_x * span_y + cell_y - 1]
    ) * 0.5
    sensors = center.shape[0]
    depth = vertical.shape[0]
    grouped = center.reshape(sensors, width_all // depth, depth)
    centred = (grouped - jnp.mean(grouped, axis=1, keepdims=True)).reshape(sensors, width_all)
    block = jnp.concatenate([centred * slope_x, centred * slope_y], axis=-1)
    ordered = jnp.zeros_like(block).at[slots[0]].set(block)
    grad_blocks = lax.all_to_all(ordered, "gx", split_axis=0, concat_axis=0, tiled=True)
    return (sample, grad_blocks)


def solution(mesh):
    placed = (
        P("gx", "gy", None),
        P("gx", "gy"),
        P("gx", "gy"),
        P(),
        P(),
        P(("gx", "gy"), None),
        P(("gx", "gy"), None),
    )
    return jax.shard_map(
        shards,
        mesh=mesh,
        in_specs=placed,
        out_specs=(P("gx", "gy", None), P(("gx", "gy"), None)),
        check_vma=False,
    )
```

profile of v0, /device:TPU:56, one launch (start us, length us, event | category | flops | bytes accessed | tf_op | source)
XLA Modules:
  0.0 192.1 jit_solution(16390854278508312670)
XLA Ops:
  0.6 0.0 copy-start
  0.6 1.0 fusion.38
  1.6 1.7 collective-permute-start.1
  3.4 1.3 collective-permute-start
  4.7 4.5 %reshape.304 = f32[8192,64]{1,0:T(8,128)} reshape(f32[16,64,512]{2,1,0:T(8,128)} %param.7) | data formatting | bytes 4194304 | tf_op jit(solution)/shard_map/reshape | solution.py:28
  9.2 6.7 %fusion.40 = f32[8192,64]{1,0:T(8,128)} fusion(f32[8192,64]{1,0:T(8,128)} %reshape.304, f32[64,64]{1,0:T(8,128)S(1)} %copy-done), kind=kOutput, calls=%fused_computation.99 | convolution fusion | flops 402653184 | bytes 4210688 | tf_op jit(solution)/shard_map/dot_general | solution.py:27
  15.9 0.0 collective-permute-done.1
  15.9 0.2 constant_dynamic-update-slice_fusion.1
  16.1 0.0 collective-permute-done
  16.2 1.4 copy-done.5
  17.6 0.1 fusion.34
  17.7 3.3 %collective-permute-start.2 = (f32[18,1,512]{2,1,0:T(1,128)S(1)}, f32[18,1,512]{2,1,0:T(1,128)S(1)}, u32[]{:S(2)}, u32[]{:S(2)}) collective-permute-start(f32[18,1,512]{2,1,0:T(1,128)S(1)} %get-tuple-element.13), channel_id=1, source_target_pairs={{1,0},{2,1},{3,2},{4,3},{5,4},{6,5},{7,6},{8,7},{9,8},{10,9},{11,1... | collective-permute-start | bytes 110600 | tf_op jit(solution)/shard_map/ppermute | solution.py:17
  20.9 6.2 %collective-permute-start.3 = (f32[18,1,512]{2,1,0:T(1,128)S(1)}, f32[18,1,512]{2,1,0:T(1,128)S(1)}, u32[]{:S(2)}, u32[]{:S(2)}) collective-permute-start(f32[18,1,512]{2,1,0:T(1,128)S(1)} %get-tuple-element.14), channel_id=1, source_target_pairs={{0,1},{1,2},{2,3},{3,4},{4,5},{5,6},{6,7},{7,8},{8,9},{9,10},{10,1... | collective-permute-start | bytes 110600 | tf_op jit(solution)/shard_map/ppermute | solution.py:15
  27.2 0.0 copy-start.6
  27.2 0.0 copy-start.7
  27.2 4.8 %reshape.305 = f32[16,64,512]{2,1,0:T(8,128)} reshape(f32[8192,64]{1,0:T(8,128)} %fusion.40) | data formatting | bytes 4194304 | tf_op jit(solution)/shard_map/reshape | solution.py:32
  32.0 4.1 %fusion.18 = f32[16,64,512]{2,1,0:T(8,128)S(1)} fusion(f32[18,64,512]{2,1,0:T(8,128)} %copy-done.5, f32[18,1,512]{2,1,0:T(1,128)S(1)} %collective-permute-done.3, f32[18,1,512]{2,1,0:T(1,128)S(1)} %collective-permute-done.2, f32[16,64,512]{2,1,0:T(8,128)S(1)} %copy-done.1, f32[1,64,512]{2,1,0:T(8,128)S(1)} %collective-permute-done.1, ...), kind=kLoop, calls=%fused_computation.42 | loop fusion | flops 5767168 | bytes 8994816 | tf_op jit(solution)/shard_map/sub | solution.py:33
  36.1 0.0 copy-start.2
  36.1 1.3 copy-done.2
  37.4 1.3 collective-permute-start.4
  38.7 5.3 %collective-permute-start.5 = (f32[1,64,512]{2,1,0:T(8,128)S(1)}, f32[1,64,512]{2,1,0:T(8,128)S(1)}, u32[]{:S(2)}, u32[]{:S(2)}) collective-permute-start(f32[1,64,512]{2,1,0:T(8,128)S(1)} %get-tuple-element.19), channel_id=1, source_target_pairs={{0,16},{16,32},{32,48},{48,64},{64,80},{80,96},{96,112},{112,128},... | collective-permute-start | bytes 393224 | tf_op jit(solution)/shard_map/ppermute | solution.py:15
  44.0 4.5 %reshape.306 = f32[8192,64]{1,0:T(8,128)} reshape(f32[16,64,512]{2,1,0:T(8,128)} %copy-done.2) | data formatting | bytes 4194304 | tf_op jit(solution)/shard_map/reshape | solution.py:28
  48.5 0.0 collective-permute-done.4
  48.5 1.1 pad_maximum_fusion.29
  49.6 1.9 %collective-permute-start.6 = (f32[18,1,512]{2,1,0:T(1,128)S(1)}, f32[18,1,512]{2,1,0:T(1,128)S(1)}, u32[]{:S(2)}, u32[]{:S(2)}) collective-permute-start(f32[18,1,512]{2,1,0:T(1,128)S(1)} %get-tuple-element.11), channel_id=1, source_target_pairs={{1,0},{2,1},{3,2},{4,3},{5,4},{6,5},{7,6},{8,7},{9,8},{10,9},{11,1... | collective-permute-start | bytes 110600 | tf_op jit(solution)/shard_map/ppermute | solution.py:17
  51.5 7.5 %collective-permute-start.7 = (f32[18,1,512]{2,1,0:T(1,128)S(1)}, f32[18,1,512]{2,1,0:T(1,128)S(1)}, u32[]{:S(2)}, u32[]{:S(2)}) collective-permute-start(f32[18,1,512]{2,1,0:T(1,128)S(1)} %get-tuple-element.12), channel_id=1, source_target_pairs={{0,1},{1,2},{2,3},{3,4},{4,5},{5,6},{6,7},{7,8},{8,9},{9,10},{10,1... | collective-permute-start | bytes 110600 | tf_op jit(solution)/shard_map/ppermute | solution.py:15
  59.1 6.5 %fusion.41 = f32[8192,64]{1,0:T(8,128)} fusion(f32[8192,64]{1,0:T(8,128)} %reshape.306, f32[64,64]{1,0:T(8,128)S(1)} %copy-done), kind=kOutput, calls=%fused_computation.100 | convolution fusion | flops 402653184 | bytes 4210688 | tf_op jit(solution)/shard_map/dot_general | solution.py:27
  65.6 4.8 %reshape.307 = f32[16,64,512]{2,1,0:T(8,128)} reshape(f32[8192,64]{1,0:T(8,128)} %fusion.41) | data formatting | bytes 4194304 | tf_op jit(solution)/shard_map/reshape | solution.py:32
  70.4 0.0 collective-permute-done.6
  70.4 7.7 %fusion.13 = f32[16,64,512]{2,1,0:T(8,128)S(1)} fusion(f32[16,64,512]{2,1,0:T(8,128)S(1)} %copy-done.1, f32[18,1,512]{2,1,0:T(1,128)S(1)} %collective-permute-done.7, f32[1,64,512]{2,1,0:T(8,128)S(1)} %collective-permute-done.4, f32[16,64,512]{2,1,0:T(8,128)} %copy-done.2, f32[1,64,512]{2,1,0:T(8,128)S(1)} %collective-permute-done.5, ...), kind=kLoop, calls=%fused_computation.29 | loop fusion | flops 8912896 | bytes 8732672 | tf_op jit(solution)/shard_map/sub | solution.py:43
  78.1 1.4 copy-done.3
  79.5 1.3 collective-permute-start.8
  80.8 4.3 %collective-permute-start.9 = (f32[1,64,512]{2,1,0:T(8,128)S(1)}, f32[1,64,512]{2,1,0:T(8,128)S(1)}, u32[]{:S(2)}, u32[]{:S(2)}) collective-permute-start(f32[1,64,512]{2,1,0:T(8,128)S(1)} %get-tuple-element.17), channel_id=1, source_target_pairs={{0,16},{16,32},{32,48},{48,64},{64,80},{80,96},{96,112},{112,128},... | collective-permute-start | bytes 393224 | tf_op jit(solution)/shard_map/ppermute | solution.py:15
  85.1 0.6 fusion.39
  85.7 4.5 %reshape.308 = f32[8192,64]{1,0:T(8,128)} reshape(f32[16,64,512]{2,1,0:T(8,128)} %copy-done.3) | data formatting | bytes 4194304 | tf_op jit(solution)/shard_map/reshape | solution.py:28
  90.2 1.1 pad_maximum_fusion.26
  91.3 1.9 %collective-permute-start.10 = (f32[18,1,512]{2,1,0:T(1,128)S(1)}, f32[18,1,512]{2,1,0:T(1,128)S(1)}, u32[]{:S(2)}, u32[]{:S(2)}) collective-permute-start(f32[18,1,512]{2,1,0:T(1,128)S(1)} %get-tuple-element.9), channel_id=1, source_target_pairs={{1,0},{2,1},{3,2},{4,3},{5,4},{6,5},{7,6},{8,7},{9,8},{10,9},{11,1... | collective-permute-start | bytes 110600 | tf_op jit(solution)/shard_map/ppermute | solution.py:17
  93.2 7.7 %collective-permute-start.11 = (f32[18,1,512]{2,1,0:T(1,128)S(1)}, f32[18,1,512]{2,1,0:T(1,128)S(1)}, u32[]{:S(2)}, u32[]{:S(2)}) collective-permute-start(f32[18,1,512]{2,1,0:T(1,128)S(1)} %get-tuple-element.10), channel_id=1, source_target_pairs={{0,1},{1,2},{2,3},{3,4},{4,5},{5,6},{6,7},{7,8},{8,9},{9,10},{10,1... | collective-permute-start | bytes 110600 | tf_op jit(solution)/shard_map/ppermute | solution.py:15
  100.9 6.5 %fusion.42 = f32[8192,64]{1,0:T(8,128)} fusion(f32[8192,64]{1,0:T(8,128)} %reshape.308, f32[64,64]{1,0:T(8,128)S(1)} %copy-done), kind=kOutput, calls=%fused_computation.101 | convolution fusion | flops 402653184 | bytes 4210688 | tf_op jit(solution)/shard_map/dot_general | solution.py:27
  107.4 4.8 %reshape.309 = f32[16,64,512]{2,1,0:T(8,128)} reshape(f32[8192,64]{1,0:T(8,128)} %fusion.42) | data formatting | bytes 4194304 | tf_op jit(solution)/shard_map/reshape | solution.py:32
  112.2 11.1 %fusion.6 = f32[16,64,512]{2,1,0:T(8,128)S(1)} fusion(f32[16,64,512]{2,1,0:T(8,128)} %copy-done.2, f32[18,1,512]{2,1,0:T(1,128)S(1)} %collective-permute-done.11, f32[1,64,512]{2,1,0:T(8,128)S(1)} %collective-permute-done.8, f32[16,64,512]{2,1,0:T(8,128)} %copy-done.3, f32[1,64,512]{2,1,0:T(8,128)S(1)} %collective-permute-done.9, ...), kind=kLoop, calls=%fused_computation.14 | loop fusion | flops 12582912 | bytes 10829840 | tf_op jit(solution)/shard_map/add | solution.py:45
  123.4 0.0 copy-start.4
  123.4 3.1 %collective-permute-start.12 = (f32[1,64,512]{2,1,0:T(8,128)S(1)}, f32[1,64,512]{2,1,0:T(8,128)S(1)}, u32[]{:S(2)}, u32[]{:S(2)}) collective-permute-start(f32[1,64,512]{2,1,0:T(8,128)S(1)} %get-tuple-element.15), channel_id=1, source_target_pairs={{0,16},{16,32},{32,48},{48,64},{64,80},{80,96},{96,112},{112,128},... | collective-permute-start | bytes 393224 | tf_op jit(solution)/shard_map/ppermute | solution.py:15
  126.5 1.3 collective-permute-start.13
  127.8 2.7 %collective-permute-done.13 = f32[1,64,512]{2,1,0:T(8,128)S(1)} collective-permute-done((f32[1,64,512]{2,1,0:T(8,128)S(1)}, f32[1,64,512]{2,1,0:T(8,128)S(1)}, u32[]{:S(2)}, u32[]{:S(2)}) %collective-permute-start.13) | collective-permute-done | bytes 131104 | tf_op jit(solution)/shard_map/ppermute | solution.py:17
  130.6 0.1 pad_maximum_fusion.23
  130.6 1.9 %collective-permute-start.14 = (f32[18,1,512]{2,1,0:T(1,128)S(1)}, f32[18,1,512]{2,1,0:T(1,128)S(1)}, u32[]{:S(2)}, u32[]{:S(2)}) collective-permute-start(f32[18,1,512]{2,1,0:T(1,128)S(1)} %get-tuple-element.7), channel_id=1, source_target_pairs={{0,1},{1,2},{2,3},{3,4},{4,5},{5,6},{6,7},{7,8},{8,9},{9,10},{10,1... | collective-permute-start | bytes 110600 | tf_op jit(solution)/shard_map/ppermute | solution.py:15
  132.5 3.9 %collective-permute-start.15 = (f32[18,1,512]{2,1,0:T(1,128)S(1)}, f32[18,1,512]{2,1,0:T(1,128)S(1)}, u32[]{:S(2)}, u32[]{:S(2)}) collective-permute-start(f32[18,1,512]{2,1,0:T(1,128)S(1)} %get-tuple-element.8), channel_id=1, source_target_pairs={{1,0},{2,1},{3,2},{4,3},{5,4},{6,5},{7,6},{8,7},{9,8},{10,9},{11,1... | collective-permute-start | bytes 110600 | tf_op jit(solution)/shard_map/ppermute | solution.py:17
  136.5 5.5 %collective-permute-done.15 = f32[18,1,512]{2,1,0:T(1,128)S(1)} collective-permute-done((f32[18,1,512]{2,1,0:T(1,128)S(1)}, f32[18,1,512]{2,1,0:T(1,128)S(1)}, u32[]{:S(2)}, u32[]{:S(2)}) %collective-permute-start.15) | collective-permute-done | bytes 36896 | tf_op jit(solution)/shard_map/ppermute | solution.py:17
  142.0 1.9 pad_maximum_fusion
  143.9 3.4 %reshape.310 = f32[1188,512]{1,0:T(8,128)} reshape(f32[18,66,512]{2,1,0:T(8,128)} %pad_maximum_fusion) | data formatting | bytes 4866048 | tf_op jit(solution)/shard_map/reshape | solution.py:50
  147.3 2.4 %gather_fusion = f32[64,512]{1,0:T(8,128)S(1)} fusion(f32[1188,512]{1,0:T(8,128)} %reshape.310, s32[1024]{0:T(1024)S(1)} %get-tuple-element.33), kind=kCustom, calls=%fused_computation | custom fusion | bytes 262400 | tf_op jit(solution)/shard_map/gather | solution.py:54
  149.7 0.1 reshape.311
  149.8 0.1 reduce_sum.9
  149.9 0.1 sub.49
  150.0 2.4 %gather_fusion.3 = f32[64,512]{1,0:T(8,128)S(1)} fusion(f32[1188,512]{1,0:T(8,128)} %reshape.310, s32[1024]{0:T(1024)S(1)} %get-tuple-element.35), kind=kCustom, calls=%fused_computation.3 | custom fusion | bytes 262400 | tf_op jit(solution)/shard_map/gather | solution.py:59
  152.4 2.4 %gather_fusion.4 = f32[64,512]{1,0:T(8,128)S(1)} fusion(f32[1188,512]{1,0:T(8,128)} %reshape.310, s32[1024]{0:T(1024)S(1)} %get-tuple-element.34), kind=kCustom, calls=%fused_computation.4 | custom fusion | bytes 262400 | tf_op jit(solution)/shard_map/gather | solution.py:59
  154.9 2.4 %gather_fusion.1 = f32[64,512]{1,0:T(8,128)S(1)} fusion(f32[1188,512]{1,0:T(8,128)} %reshape.310, s32[1024]{0:T(1024)S(1)} %get-tuple-element.32), kind=kCustom, calls=%fused_computation.1 | custom fusion | bytes 262400 | tf_op jit(solution)/shard_map/gather | solution.py:56
  157.3 2.4 %gather_fusion.2 = f32[64,512]{1,0:T(8,128)S(1)} fusion(f32[1188,512]{1,0:T(8,128)} %reshape.310, s32[1024]{0:T(1024)S(1)} %pad_clamp_fusion.2), kind=kCustom, calls=%fused_computation.2 | custom fusion | bytes 262400 | tf_op jit(solution)/shard_map/gather | solution.py:56
  159.7 0.1 multiply_multiply_fusion.1
  159.7 0.9 scatter_custom_fusion
  160.6 0.1 all_to_all.8
  160.8 30.4 %all_to_all.12 = f32[32,2,1024]{2,1,0:T(2,128)S(1)} all-to-all(f32[32,2,1024]{2,1,0:T(2,128)S(1)} %all_to_all.8), channel_id=1, replica_groups=mesh['gx'=32,'gy'=16] {'gx'}, dimensions={0} | all-to-all | bytes 524288 | tf_op jit(solution)/shard_map/all_to_all | solution.py:67
  191.2 0.9 all_to_all.10
  (38 shorter events, 0.2 us)
Async XLA Ops:
  0.6 8.6 %copy-start = (f32[64,64]{1,0:T(8,128)S(1)}, f32[64,64]{1,0:T(8,128)}, u32[]{:S(2)}) copy-start(f32[64,64]{1,0:T(8,128)} %param.10) | copy-start | bytes 49156
  1.6 14.2 %collective-permute-start.1 = (f32[1,64,512]{2,1,0:T(8,128)S(1)}, f32[1,64,512]{2,1,0:T(8,128)S(1)}, u32[]{:S(2)}, u32[]{:S(2)}) collective-permute-start(f32[1,64,512]{2,1,0:T(8,128)S(1)} %get-tuple-element.22), channel_id=1, source_target_pairs={{0,16},{16,32},{32,48},{48,64},{64,80},{80,96},{96,112},{112,128},... | collective-permute-start | bytes 393224 | tf_op jit(solution)/shard_map/ppermute | solution.py:15
  3.4 12.7 %collective-permute-start = (f32[1,64,512]{2,1,0:T(8,128)S(1)}, f32[1,64,512]{2,1,0:T(8,128)S(1)}, u32[]{:S(2)}, u32[]{:S(2)}) collective-permute-start(f32[1,64,512]{2,1,0:T(8,128)S(1)} %get-tuple-element.21), channel_id=1, source_target_pairs={{16,0},{32,16},{48,32},{64,48},{80,64},{96,80},{112,96},{128,112},... | collective-permute-start | bytes 393224 | tf_op jit(solution)/shard_map/ppermute | solution.py:17
  9.2 6.7 %copy-start.9 = (s32[1,64]{1,0:T(1,128)S(1)}, s32[1,64]{1,0:T(1,128)}, u32[]{:S(2)}) copy-start(s32[1,64]{1,0:T(1,128)} %param.12) | copy-start | bytes 772
  9.2 6.7 %copy-start.1 = (f32[16,64,512]{2,1,0:T(8,128)S(1)}, f32[16,64,512]{2,1,0:T(8,128)}, u32[]{:S(2)}) copy-start(f32[16,64,512]{2,1,0:T(8,128)} %param.7) | copy-start | bytes 6291460
  16.2 1.4 copy-start.5
  17.7 14.3 %collective-permute-start.2 = (f32[18,1,512]{2,1,0:T(1,128)S(1)}, f32[18,1,512]{2,1,0:T(1,128)S(1)}, u32[]{:S(2)}, u32[]{:S(2)}) collective-permute-start(f32[18,1,512]{2,1,0:T(1,128)S(1)} %get-tuple-element.13), channel_id=1, source_target_pairs={{1,0},{2,1},{3,2},{4,3},{5,4},{6,5},{7,6},{8,7},{9,8},{10,9},{11,1... | collective-permute-start | bytes 110600 | tf_op jit(solution)/shard_map/ppermute | solution.py:17
  20.9 11.0 %collective-permute-start.3 = (f32[18,1,512]{2,1,0:T(1,128)S(1)}, f32[18,1,512]{2,1,0:T(1,128)S(1)}, u32[]{:S(2)}, u32[]{:S(2)}) collective-permute-start(f32[18,1,512]{2,1,0:T(1,128)S(1)} %get-tuple-element.14), channel_id=1, source_target_pairs={{0,1},{1,2},{2,3},{3,4},{4,5},{5,6},{6,7},{7,8},{8,9},{9,10},{10,1... | collective-permute-start | bytes 110600 | tf_op jit(solution)/shard_map/ppermute | solution.py:15
  27.2 4.8 %copy-start.6 = (f32[16,64]{1,0:T(8,128)S(1)}, f32[16,64]{1,0:T(8,128)}, u32[]{:S(2)}) copy-start(f32[16,64]{1,0:T(8,128)} %param.9) | copy-start | bytes 12292
  27.2 4.8 %copy-start.7 = (f32[16,64]{1,0:T(8,128)S(1)}, f32[16,64]{1,0:T(8,128)}, u32[]{:S(2)}) copy-start(f32[16,64]{1,0:T(8,128)} %param.8) | copy-start | bytes 12292
  36.1 1.3 copy-start.2
  37.4 11.1 %collective-permute-start.4 = (f32[1,64,512]{2,1,0:T(8,128)S(1)}, f32[1,64,512]{2,1,0:T(8,128)S(1)}, u32[]{:S(2)}, u32[]{:S(2)}) collective-permute-start(f32[1,64,512]{2,1,0:T(8,128)S(1)} %get-tuple-element.20), channel_id=1, source_target_pairs={{16,0},{32,16},{48,32},{64,48},{80,64},{96,80},{112,96},{128,112},... | collective-permute-start | bytes 393224 | tf_op jit(solution)/shard_map/ppermute | solution.py:17
  38.7 9.8 %collective-permute-start.5 = (f32[1,64,512]{2,1,0:T(8,128)S(1)}, f32[1,64,512]{2,1,0:T(8,128)S(1)}, u32[]{:S(2)}, u32[]{:S(2)}) collective-permute-start(f32[1,64,512]{2,1,0:T(8,128)S(1)} %get-tuple-element.19), channel_id=1, source_target_pairs={{0,16},{16,32},{32,48},{48,64},{64,80},{80,96},{96,112},{112,128},... | collective-permute-start | bytes 393224 | tf_op jit(solution)/shard_map/ppermute | solution.py:15
  49.6 20.8 %collective-permute-start.6 = (f32[18,1,512]{2,1,0:T(1,128)S(1)}, f32[18,1,512]{2,1,0:T(1,128)S(1)}, u32[]{:S(2)}, u32[]{:S(2)}) collective-permute-start(f32[18,1,512]{2,1,0:T(1,128)S(1)} %get-tuple-element.11), channel_id=1, source_target_pairs={{1,0},{2,1},{3,2},{4,3},{5,4},{6,5},{7,6},{8,7},{9,8},{10,9},{11,1... | collective-permute-start | bytes 110600 | tf_op jit(solution)/shard_map/ppermute | solution.py:17
  51.5 18.9 %collective-permute-start.7 = (f32[18,1,512]{2,1,0:T(1,128)S(1)}, f32[18,1,512]{2,1,0:T(1,128)S(1)}, u32[]{:S(2)}, u32[]{:S(2)}) collective-permute-start(f32[18,1,512]{2,1,0:T(1,128)S(1)} %get-tuple-element.12), channel_id=1, source_target_pairs={{0,1},{1,2},{2,3},{3,4},{4,5},{5,6},{6,7},{7,8},{8,9},{9,10},{10,1... | collective-permute-start | bytes 110600 | tf_op jit(solution)/shard_map/ppermute | solution.py:15
  70.4 14.7 %copy-start.10 = (s32[1,64]{1,0:T(1,128)S(1)}, s32[1,64]{1,0:T(1,128)}, u32[]{:S(2)}) copy-start(s32[1,64]{1,0:T(1,128)} %param.13) | copy-start | bytes 772
  70.4 14.7 %copy-start.8 = (f32[4]{0:T(128)S(1)}, f32[4]{0:T(128)}, u32[]{:S(2)}) copy-start(f32[4]{0:T(128)} %param.11) | copy-start | bytes 52
  78.1 1.4 copy-start.3
  79.5 10.7 %collective-permute-start.8 = (f32[1,64,512]{2,1,0:T(8,128)S(1)}, f32[1,64,512]{2,1,0:T(8,128)S(1)}, u32[]{:S(2)}, u32[]{:S(2)}) collective-permute-start(f32[1,64,512]{2,1,0:T(8,128)S(1)} %get-tuple-element.18), channel_id=1, source_target_pairs={{16,0},{32,16},{48,32},{64,48},{80,64},{96,80},{112,96},{128,112},... | collective-permute-start | bytes 393224 | tf_op jit(solution)/shard_map/ppermute | solution.py:17
  80.8 9.4 %collective-permute-start.9 = (f32[1,64,512]{2,1,0:T(8,128)S(1)}, f32[1,64,512]{2,1,0:T(8,128)S(1)}, u32[]{:S(2)}, u32[]{:S(2)}) collective-permute-start(f32[1,64,512]{2,1,0:T(8,128)S(1)} %get-tuple-element.17), channel_id=1, source_target_pairs={{0,16},{16,32},{32,48},{48,64},{64,80},{80,96},{96,112},{112,128},... | collective-permute-start | bytes 393224 | tf_op jit(solution)/shard_map/ppermute | solution.py:15
  91.3 21.0 %collective-permute-start.10 = (f32[18,1,512]{2,1,0:T(1,128)S(1)}, f32[18,1,512]{2,1,0:T(1,128)S(1)}, u32[]{:S(2)}, u32[]{:S(2)}) collective-permute-start(f32[18,1,512]{2,1,0:T(1,128)S(1)} %get-tuple-element.9), channel_id=1, source_target_pairs={{1,0},{2,1},{3,2},{4,3},{5,4},{6,5},{7,6},{8,7},{9,8},{10,9},{11,1... | collective-permute-start | bytes 110600 | tf_op jit(solution)/shard_map/ppermute | solution.py:17
  93.2 19.0 %collective-permute-start.11 = (f32[18,1,512]{2,1,0:T(1,128)S(1)}, f32[18,1,512]{2,1,0:T(1,128)S(1)}, u32[]{:S(2)}, u32[]{:S(2)}) collective-permute-start(f32[18,1,512]{2,1,0:T(1,128)S(1)} %get-tuple-element.10), channel_id=1, source_target_pairs={{0,1},{1,2},{2,3},{3,4},{4,5},{5,6},{6,7},{7,8},{8,9},{9,10},{10,1... | collective-permute-start | bytes 110600 | tf_op jit(solution)/shard_map/ppermute | solution.py:15
  123.4 18.7 %copy-start.4 = (f32[16,64,512]{2,1,0:T(8,128)}, f32[16,64,512]{2,1,0:T(8,128)S(1)}, u32[]{:S(2)}) copy-start(f32[16,64,512]{2,1,0:T(8,128)S(1)} %fusion.6) | copy-start | bytes 6291460
  123.4 4.4 %collective-permute-start.12 = (f32[1,64,512]{2,1,0:T(8,128)S(1)}, f32[1,64,512]{2,1,0:T(8,128)S(1)}, u32[]{:S(2)}, u32[]{:S(2)}) collective-permute-start(f32[1,64,512]{2,1,0:T(8,128)S(1)} %get-tuple-element.15), channel_id=1, source_target_pairs={{0,16},{16,32},{32,48},{48,64},{64,80},{80,96},{96,112},{112,128},... | collective-permute-start | bytes 393224 | tf_op jit(solution)/shard_map/ppermute | solution.py:15
  126.5 4.1 %collective-permute-start.13 = (f32[1,64,512]{2,1,0:T(8,128)S(1)}, f32[1,64,512]{2,1,0:T(8,128)S(1)}, u32[]{:S(2)}, u32[]{:S(2)}) collective-permute-start(f32[1,64,512]{2,1,0:T(8,128)S(1)} %get-tuple-element.16), channel_id=1, source_target_pairs={{16,0},{32,16},{48,32},{64,48},{80,64},{96,80},{112,96},{128,112},... | collective-permute-start | bytes 393224 | tf_op jit(solution)/shard_map/ppermute | solution.py:17
  130.6 5.9 %collective-permute-start.14 = (f32[18,1,512]{2,1,0:T(1,128)S(1)}, f32[18,1,512]{2,1,0:T(1,128)S(1)}, u32[]{:S(2)}, u32[]{:S(2)}) collective-permute-start(f32[18,1,512]{2,1,0:T(1,128)S(1)} %get-tuple-element.7), channel_id=1, source_target_pairs={{0,1},{1,2},{2,3},{3,4},{4,5},{5,6},{6,7},{7,8},{8,9},{9,10},{10,1... | collective-permute-start | bytes 110600 | tf_op jit(solution)/shard_map/ppermute | solution.py:15
  132.5 9.5 %collective-permute-start.15 = (f32[18,1,512]{2,1,0:T(1,128)S(1)}, f32[18,1,512]{2,1,0:T(1,128)S(1)}, u32[]{:S(2)}, u32[]{:S(2)}) collective-permute-start(f32[18,1,512]{2,1,0:T(1,128)S(1)} %get-tuple-element.8), channel_id=1, source_target_pairs={{1,0},{2,1},{3,2},{4,3},{5,4},{6,5},{7,6},{8,7},{9,8},{10,9},{11,1... | collective-permute-start | bytes 110600 | tf_op jit(solution)/shard_map/ppermute | solution.py:17
where the time goes:
time: 193 us; the launch traced here: 192 us
  starting transfers between devices  53.9 us (28%)
  local copies, waits for them, and re-layouts  50.6 us (26%)
  blocking collectives  30.4 us (16%)
  other arithmetic  28.1 us (15%)
  matrix products  19.7 us (10%)
  waiting for transfers between devices  8.27 us (4%)
    ppermute x8, starting transfers between devices, with_halo(): lax.ppermute(tail, axis, [(i, (i + 1) % count) for i in range(ends)])  37.7 us
    all_to_all x1, blocking collectives, shards(): lax.all_to_all(ordered, 'gx', split_axis=0, concat_axis=0, tiled=True)  30.4 us
    dot_general x3, matrix products, operate(): jnp.dot(core.reshape(-1, vertical.shape[0]), vertical.T, precision=lax.Pr...  19.7 us
    ppermute x8, starting transfers between devices, with_halo(): lax.ppermute(head, axis, [((i + 1) % count, i) for i in range(ends)])  16.2 us
    reshape x3, local copies, waits for them, and re-layouts, operate(): column = jnp.dot(core.reshape(-1, vertical.shape[0]), vertical.T, precisi...  14.3 us
    reshape x3, local copies, waits for them, and re-layouts, operate(): core.reshape(-1, vertical.shape[0])  13.5 us
    add x1, other arithmetic, shards(): coeffs[0] * noise + coeffs[1] * first + coeffs[2] * second  11.1 us
    ppermute x8, waiting for transfers between devices, with_halo(): lax.ppermute(head, axis, [((i + 1) % count, i) for i in range(ends)])  8.25 us
  transfers between devices with their start and end apart: 16, of which 2 were waited for; matrix products, arithmetic and copies ran while one was open for 25% of the time, Pallas kernels for 0%

commit v1 on v0

v1 whole, which is shorter than its diff:
```python
import functools

import jax
import jax.numpy as jnp
from jax import lax
from jax.experimental import pallas as pl
from jax.experimental.pallas import tpu as pltpu
from jax.sharding import PartitionSpec as P

MESH = pl.DeviceIdType.MESH
HIGHEST = lax.Precision.HIGHEST
F32 = jnp.float32
BF16 = jnp.bfloat16
LANES = 128
PAD = 8


def split2(value):
    high = value.astype(BF16)
    return high, (value - high.astype(F32)).astype(BF16)


def iota(shape, dim):
    return lax.broadcasted_iota(jnp.int32, shape, dim)


def dot_t(a, b):
    return lax.dot_general(a, b, (((1,), (1,)), ((), ())), precision=HIGHEST, preferred_element_type=F32)


def dot(a, b):
    return jnp.dot(a, b, precision=HIGHEST, preferred_element_type=F32)


def kernel(n_gx, n_gy, noise, rate, coupling, vertical, slots, columns, coeffs, sample, grads,
           e0, e1, e2, e3, rate_b, coup_b, weights, y_out, y_in, g_c, g_x, g_y, ready,
           load_sem, xs_sem, xr_sem, ys_sem, yr_sem, as_sem, ar_sem, store_sem, own_sem):
    cx, cy, width = noise.shape
    depth = vertical.shape[0]
    sensors = slots.shape[1]
    reps = width // LANES
    me = lax.axis_index("gx")
    my = lax.axis_index("gy")
    fields = (e0, e1, e2, e3)
    own = pl.ds(PAD, cy)

    barrier = pltpu.get_barrier_semaphore()

    def greet(k, carry):
        pl.semaphore_signal(barrier, inc=1, device_id=(lax.rem(me + k, n_gx), my), device_id_type=MESH)
        return carry

    lax.fori_loop(1, n_gx, greet, 0)

    @pl.when(my > 0)
    def _():
        pl.semaphore_signal(barrier, inc=1, device_id=(me, my - 1), device_id_type=MESH)

    @pl.when(my < n_gy - 1)
    def _():
        pl.semaphore_signal(barrier, inc=1, device_id=(me, my + 1), device_id_type=MESH)

    load = pltpu.make_async_copy(noise, e0.at[pl.ds(1, cx), own, :], load_sem)
    load.start()

    zero_row = jnp.zeros((cy, width), F32)
    zero_col = jnp.zeros((cx, width), F32)

    @pl.when(me == 0)
    def _():
        for field in fields:
            field[0, own, :] = zero_row

    @pl.when(me == n_gx - 1)
    def _():
        for field in fields:
            field[cx + 1, own, :] = zero_row

    @pl.when(my == 0)
    def _():
        for r in range(4):
            y_in[r, 0] = zero_col

    @pl.when(my == n_gy - 1)
    def _():
        for r in range(4):
            y_in[r, 1] = zero_col

    diag = iota((cy, cy), 0) == iota((cy, cy), 1)

    def spread(i, carry):
        for src, dst in ((rate, rate_b), (coupling, coup_b)):
            row = jnp.broadcast_to(src[pl.ds(i, 1), :], (cy, cy))
            col = jnp.sum(jnp.where(diag, row, 0.0), axis=1, keepdims=True)
            dst[i] = jnp.broadcast_to(col, (cy, LANES))
        return carry

    lax.fori_loop(0, cx, spread, 0)

    pl.semaphore_wait(barrier, n_gx - 1 + jnp.where(my > 0, 1, 0) + jnp.where(my < n_gy - 1, 1, 0))

    def x_copy(r, side):
        src_row = 1 if side == 0 else cx
        src = fields[r].at[src_row, own, :]
        if r == 0:
            src = noise.at[src_row - 1]
        return pltpu.make_async_remote_copy(
            src_ref=src, dst_ref=fields[r].at[cx + 1 if side == 0 else 0, own, :],
            send_sem=xs_sem.at[r, side], recv_sem=xr_sem.at[r, side],
            device_id=(me - 1 if side == 0 else me + 1, my), device_id_type=MESH)

    def y_copy(r, side):
        return pltpu.make_async_remote_copy(
            src_ref=y_out.at[r, side], dst_ref=y_in.at[r, 1 - side],
            send_sem=ys_sem.at[r, side], recv_sem=yr_sem.at[r, side],
            device_id=(me, my - 1 if side == 0 else my + 1), device_id_type=MESH)

    x_has = (me > 0, me < n_gx - 1)
    y_has = (my > 0, my < n_gy - 1)

    def send_x(r):
        for side in range(2):
            @pl.when(x_has[side])
            def _():
                x_copy(r, side).start()

    def send_y(r):
        field = fields[r]
        for i in range(cx):
            y_out[r, 0, i:i + 1, :] = field[i + 1, PAD:PAD + 1, :]
            y_out[r, 1, i:i + 1, :] = field[i + 1, PAD + cy - 1:PAD + cy, :]
        for side in range(2):
            @pl.when(y_has[side])
            def _():
                y_copy(r, side).start()

    def receive(r):
        field = fields[r]
        for side in range(2):
            @pl.when(y_has[1 - side])
            def _():
                y_copy(r, side).wait_recv()
        for i in range(cx):
            field[i + 1, PAD - 1:PAD, :] = y_in[r, 0, i:i + 1, :]
            field[i + 1, PAD + cy:PAD + cy + 1, :] = y_in[r, 1, i:i + 1, :]
        for side in range(2):
            @pl.when(x_has[1 - side])
            def _():
                x_copy(r, side).wait_recv()

    def sent(r):
        for side in range(2):
            @pl.when(x_has[side])
            def _():
                x_copy(r, side).wait_send()

            @pl.when(y_has[side])
            def _():
                y_copy(r, side).wait_send()

    q0 = coeffs[0] - coeffs[2]
    q1 = coeffs[1] - 3.0 * coeffs[3]
    q2 = 2.0 * coeffs[2]
    q3 = 4.0 * coeffs[3]

    def lateral(r, i, low, high):
        old, new = fields[r], fields[r + 1]
        rows = pl.ds(PAD + low, high - low)
        beside = (old[i, rows, :] + old[i + 2, rows, :]) + (
            old[i + 1, PAD - 1 + low:PAD - 1 + high, :] + old[i + 1, PAD + 1 + low:PAD + 1 + high, :])
        a = rate_b[i, low:high, :]
        b = coup_b[i, low:high, :]
        if r == 0:
            a, b = q3 * a, q3 * b
        a = jnp.concatenate([a] * reps, axis=1)
        b = jnp.concatenate([b] * reps, axis=1)
        new[i + 1, rows, :] = new[i + 1, rows, :] + a * old[i + 1, rows, :] - b * beside

    def inner(r):
        def row(i, carry):
            lateral(r, i, 8, cy - 8)
            return carry

        lax.fori_loop(1, cx - 1, row, 0)

    def outer(r):
        lateral(r, 0, 0, cy)
        lateral(r, cx - 1, 0, cy)

        def row(i, carry):
            lateral(r, i, 0, 8)
            lateral(r, i, cy - 8, cy)
            return carry

        lax.fori_loop(1, cx - 1, row, 0)

    send_x(0)
    load.wait()
    send_y(0)

    block = 2 * LANES
    pick = (iota((block, depth), 0) % depth == iota((block, depth), 1)).astype(F32)
    tiled = dot_t(dot_t(pick, vertical[...]), pick)
    same = iota((block, block), 0) // depth == iota((block, block), 1) // depth
    eye = jnp.where(iota((block, block), 0) == iota((block, block), 1), 1.0, 0.0)
    v1 = jnp.where(same, tiled, 0.0)
    v2 = dot(v1, v1)
    v3 = dot(v1, v2)
    polys = (
        q2 * eye + (3.0 * q3) * v1,
        q1 * eye + (2.0 * q2) * v1 + (3.0 * q3) * v2,
        q0 * eye + q1 * v1 + q2 * v2 + q3 * v3,
    )
    for k, poly in enumerate(polys):
        high, low = split2(poly)
        weights[k, 0:block, :] = high
        weights[k, block:2 * block, :] = high
        weights[k, 2 * block:3 * block, :] = low

    group = 4

    def columns_of(k):
        def part(g, carry):
            rows = pl.ds(1 + g * group, group)
            for half in range(width // block):
                lanes = slice(half * block, (half + 1) * block)
                high, low = split2(e0[rows, own, lanes].reshape(group * cy, block))
                out = jnp.dot(jnp.concatenate([high, low, high], axis=1), weights[k],
                              preferred_element_type=F32)
                fields[k + 1][rows, own, lanes] = out.reshape(group, cy, block)
            return carry

        lax.fori_loop(0, cx // group, part, 0)

    columns_of(0)
    inner(0)
    receive(0)
    outer(0)
    send_x(1)
    send_y(1)
    columns_of(1)
    inner(1)
    receive(1)
    outer(1)
    send_x(2)
    send_y(2)
    columns_of(2)
    inner(2)
    receive(2)
    outer(2)
    send_x(3)
    send_y(3)
    store = pltpu.make_async_copy(e3.at[pl.ds(1, cx), own, :], sample, store_sem)
    store.start()
    receive(3)

    def gather(k, carry):
        place = columns[0, k]
        i = place // cy
        j = place % cy + PAD
        spot = pl.ds(k, 1)
        g_c[spot, :] = e3[i + 1, pl.ds(j, 1), :]
        g_x[spot, :] = (e3[i + 2, pl.ds(j, 1), :] - e3[i, pl.ds(j, 1), :]) * 0.5
        g_y[spot, :] = (e3[i + 1, pl.ds(j + 1, 1), :] - e3[i + 1, pl.ds(j - 1, 1), :]) * 0.5
        return carry

    lax.fori_loop(0, sensors, gather, 0, unroll=4)

    draws = width // depth
    center = g_c[...]
    total = center[:, 0:LANES]
    for t in range(1, reps):
        total = total + center[:, t * LANES:(t + 1) * LANES]
    total = (total + pltpu.roll(total, depth, axis=1)) * (1.0 / draws)
    to_slot = (iota((sensors, sensors), 0) == slots[...]).astype(BF16)
    for d, slope in enumerate((g_x, g_y)):
        for t in range(reps):
            lanes = slice(t * LANES, (t + 1) * LANES)
            value = (center[:, lanes] - total) * slope[:, lanes]
            first = value.astype(BF16)
            rest = value - first.astype(F32)
            second, third = split2(rest)
            out = (jnp.dot(to_slot, first, preferred_element_type=F32)
                   + jnp.dot(to_slot, second, preferred_element_type=F32)
                   + jnp.dot(to_slot, third, preferred_element_type=F32))
            ready[pl.ds(d * reps + t, sensors, stride=2 * reps), :] = out

    per = ready.shape[0] // n_gx
    spot = pl.ds(pl.multiple_of(me * per, per), per)

    def to_peer(k):
        peer = lax.rem(me + k, n_gx)
        return pltpu.make_async_remote_copy(
            src_ref=ready.at[pl.ds(pl.multiple_of(peer * per, per), per), :], dst_ref=grads.at[spot, :],
            send_sem=as_sem.at[k], recv_sem=ar_sem.at[k], device_id=(peer, my), device_id_type=MESH)

    def start(k, carry):
        to_peer(k).start()
        return carry

    lax.fori_loop(1, n_gx, start, 0)
    keep = pltpu.make_async_copy(ready.at[spot, :], grads.at[spot, :], own_sem)
    keep.start()
    for r in range(4):
        sent(r)
    store.wait()
    keep.wait()

    def finish(k, carry):
        copy = to_peer(k)
        copy.wait_send()
        copy.wait_recv()
        return carry

    lax.fori_loop(1, n_gx, finish, 0)


def shards(n_gx, n_gy, noise, rate, coupling, vertical, coeffs, columns, slots):
    cx, cy, width = noise.shape
    sensors = slots.shape[1]
    parts = 2 * width // LANES
    vmem = pl.BlockSpec(memory_space=pltpu.VMEM)
    smem = pl.BlockSpec(memory_space=pltpu.SMEM)
    hbm = pl.BlockSpec(memory_space=pl.ANY)
    field = pltpu.VMEM((cx + 2, cy + 2 * PAD, width), F32)
    dma = pltpu.SemaphoreType.DMA
    sample, grads = pl.pallas_call(
        functools.partial(kernel, n_gx, n_gy),
        out_shape=(jax.ShapeDtypeStruct(noise.shape, F32),
                   jax.ShapeDtypeStruct((sensors * parts, LANES), F32)),
        in_specs=[hbm, vmem, vmem, vmem, vmem, smem, smem],
        out_specs=(hbm, hbm),
        scratch_shapes=[
            field, field, field, field,
            pltpu.VMEM((cx, cy, LANES), F32), pltpu.VMEM((cx, cy, LANES), F32),
            pltpu.VMEM((3, 6 * LANES, 2 * LANES), BF16),
            pltpu.VMEM((4, 2, cx, width), F32), pltpu.VMEM((4, 2, cx, width), F32),
            pltpu.VMEM((sensors, width), F32), pltpu.VMEM((sensors, width), F32), pltpu.VMEM((sensors, width), F32),
            pltpu.VMEM((sensors * parts, LANES), F32),
            dma, dma((4, 2)), dma((4, 2)), dma((4, 2)), dma((4, 2)),
            dma((n_gx,)), dma((n_gx,)), dma, dma,
        ],
        compiler_params=pltpu.CompilerParams(
            collective_id=0, has_side_effects=True, vmem_limit_bytes=40 << 20),
    )(noise, rate, coupling, vertical, slots, columns, coeffs)
    return sample, grads.reshape(sensors, parts * LANES)


def solution(mesh):
    placed = (
        P("gx", "gy", None),
        P("gx", "gy"),
        P("gx", "gy"),
        P(),
        P(),
        P(("gx", "gy"), None),
        P(("gx", "gy"), None),
    )
    return jax.shard_map(
        functools.partial(shards, mesh.shape["gx"], mesh.shape["gy"]),
        mesh=mesh,
        in_specs=placed,
        out_specs=(P("gx", "gy", None), P(("gx", "gy"), None)),
        check_vma=False,
    )
```

time: 193 us -> 52.2 us (0.27)
  the two profiles are of different devices: /device:TPU:56 before, /device:TPU:7 now
where the time goes in v1:
time: 52.2 us; the launch traced here: 51.9 us
  Pallas kernels  43.5 us (83%)
  local copies, waits for them, and re-layouts  7.77 us (15%)
  between operations  0.66 us (1%)
    pallas_call x1, Pallas kernels, shards(): pl.pallas_call(functools.partial(kernel, n_gx, n_gy), out_shape=(jax.Shap...  43.5 us
    unnamed x15, local copies, waits for them, and re-layouts  7.02 us

profile of v1, /device:TPU:7, one launch (start us, length us, event | category | flops | bytes accessed | tf_op | source)
XLA Modules:
  0.0 51.9 jit_solution(7308355991976915315)
XLA Ops:
  0.6 0.0 copy-start
  0.6 1.6 %copy-done = f32[16,64,512]{2,1,0:T(8,128)S(1)} copy-done((f32[16,64,512]{2,1,0:T(8,128)S(1)}, f32[16,64,512]{2,1,0:T(8,128)}, u32[]{:S(2)}) %copy-start) | copy-done | bytes 2097176
  2.2 0.0 copy-start.1
  2.2 0.8 %copy-done.1 = f32[64,64]{1,0:T(8,128)S(1)} copy-done((f32[64,64]{1,0:T(8,128)S(1)}, f32[64,64]{1,0:T(8,128)}, u32[]{:S(2)}) %copy-start.1) | copy-done | bytes 16408
  3.0 0.0 copy-start.2
  3.0 0.7 %copy-done.2 = f32[16,64]{1,0:T(8,128)S(1)} copy-done((f32[16,64]{1,0:T(8,128)S(1)}, f32[16,64]{1,0:T(8,128)}, u32[]{:S(2)}) %copy-start.2) | copy-done | bytes 4120
  3.7 0.0 copy-start.3
  3.7 0.7 %copy-done.3 = f32[16,64]{1,0:T(8,128)S(1)} copy-done((f32[16,64]{1,0:T(8,128)S(1)}, f32[16,64]{1,0:T(8,128)}, u32[]{:S(2)}) %copy-start.3) | copy-done | bytes 4120
  4.4 0.0 copy-start.4
  4.4 0.7 %copy-done.4 = s32[1,64]{1,0:T(1,128)S(1)} copy-done((s32[1,64]{1,0:T(1,128)S(1)}, s32[1,64]{1,0:T(1,128)}, u32[]{:S(2)}) %copy-start.4) | copy-done | bytes 280
  5.0 0.0 copy-start.5
  5.0 0.7 %copy-done.5 = s32[1,64]{1,0:T(1,128)S(1)} copy-done((s32[1,64]{1,0:T(1,128)S(1)}, s32[1,64]{1,0:T(1,128)}, u32[]{:S(2)}) %copy-start.5) | copy-done | bytes 280
  5.7 0.0 copy-start.6
  5.7 0.7 %copy-done.6 = f32[4]{0:T(128)S(1)} copy-done((f32[4]{0:T(128)S(1)}, f32[4]{0:T(128)}, u32[]{:S(2)}) %copy-start.6) | copy-done | bytes 40
  6.3 43.5 %shard_map.86 = (f32[16,64,512]{2,1,0:T(8,128)S(1)}, f32[512,128]{1,0:T(8,128)S(1)}) custom-call(f32[16,64,512]{2,1,0:T(8,128)S(1)} %copy-done, f32[16,64]{1,0:T(8,128)S(1)} %copy-done.2, f32[16,64]{1,0:T(8,128)S(1)} %copy-done.3, f32[64,64]{1,0:T(8,128)S(1)} %copy-done.1, s32[1,64]{1,0:T(1,128)S(1)} %copy-done.4, s32[1,64]{1,0:T(1,128)S(1)} %copy-done.5, ...), custom_call_target="tpu_custom_call" | custom-call | tf_op jit(solution)/shard_map/pallas_call | solution.py:327
  49.8 0.7 %reshape.7 = f32[64,1024]{1,0:T(8,128)} reshape(f32[512,128]{1,0:T(8,128)S(1)} %get-tuple-element.5) | data formatting | bytes 524288 | tf_op jit(solution)/shard_map/reshape | solution.py:346
  50.6 1.3 %copy.10 = f32[16,64,512]{2,1,0:T(8,128)} copy(f32[16,64,512]{2,1,0:T(8,128)S(1)} %get-tuple-element.8) | data formatting | bytes 4194304
Async XLA Ops:
  0.6 1.6 %copy-start = (f32[16,64,512]{2,1,0:T(8,128)S(1)}, f32[16,64,512]{2,1,0:T(8,128)}, u32[]{:S(2)}) copy-start(f32[16,64,512]{2,1,0:T(8,128)} %noise.1) | copy-start | bytes 6291460
  2.2 0.8 %copy-start.1 = (f32[64,64]{1,0:T(8,128)S(1)}, f32[64,64]{1,0:T(8,128)}, u32[]{:S(2)}) copy-start(f32[64,64]{1,0:T(8,128)} %vertical.1) | copy-start | bytes 49156
  3.0 0.7 %copy-start.2 = (f32[16,64]{1,0:T(8,128)S(1)}, f32[16,64]{1,0:T(8,128)}, u32[]{:S(2)}) copy-start(f32[16,64]{1,0:T(8,128)} %rate.1) | copy-start | bytes 12292
  3.7 0.7 %copy-start.3 = (f32[16,64]{1,0:T(8,128)S(1)}, f32[16,64]{1,0:T(8,128)}, u32[]{:S(2)}) copy-start(f32[16,64]{1,0:T(8,128)} %coupling.1) | copy-start | bytes 12292
  4.4 0.7 %copy-start.4 = (s32[1,64]{1,0:T(1,128)S(1)}, s32[1,64]{1,0:T(1,128)}, u32[]{:S(2)}) copy-start(s32[1,64]{1,0:T(1,128)} %slots.1) | copy-start | bytes 772
  5.0 0.7 %copy-start.5 = (s32[1,64]{1,0:T(1,128)S(1)}, s32[1,64]{1,0:T(1,128)}, u32[]{:S(2)}) copy-start(s32[1,64]{1,0:T(1,128)} %columns.1) | copy-start | bytes 772
  5.7 0.7 %copy-start.6 = (f32[4]{0:T(128)S(1)}, f32[4]{0:T(128)}, u32[]{:S(2)}) copy-start(f32[4]{0:T(128)} %coeffs.1) | copy-start | bytes 52

commit v2 on v1

v2 whole, which is shorter than its diff:
```python
import functools

import jax
import jax.numpy as jnp
from jax import lax
from jax.experimental import pallas as pl
from jax.experimental.pallas import tpu as pltpu
from jax.sharding import PartitionSpec as P

MESH = pl.DeviceIdType.MESH
HIGHEST = lax.Precision.HIGHEST
F32 = jnp.float32
BF16 = jnp.bfloat16
LANES = 128
GROUP = 4
PAD = 16


def split2(value):
    high = value.astype(BF16)
    return high, (value - high.astype(F32)).astype(BF16)


def iota(shape, dim):
    return lax.broadcasted_iota(jnp.int32, shape, dim)


def dot_t(a, b):
    return lax.dot_general(a, b, (((1,), (1,)), ((), ())), precision=HIGHEST, preferred_element_type=F32)


def dot(a, b):
    return jnp.dot(a, b, precision=HIGHEST, preferred_element_type=F32)


def kernel(n_gx, n_gy, noise, rate_in, coupling_in, vertical_in, slots_in, columns_in, coeffs_in, sample, grads,
           rate, coupling, vertical, slots, columns, coeffs, e0, e1, e2, e3, total, rate_b, coup_b, weights,
           y_out, y_in, beside_coef, spots_v, spots, g_c, ready,
           small_sem, load_sem, xs_sem, xr_sem, ys_sem, yr_sem, cs_sem, cr_sem, ks_sem, kr_sem, as_sem, ar_sem, store_sem, own_sem, spot_sem):
    cx, cy, width = noise.shape
    depth = vertical.shape[0]
    sensors = slots.shape[1]
    reps = width // LANES
    me = lax.axis_index("gx")
    my = lax.axis_index("gy")
    fields = (e0, e1, e2, e3)
    own = pl.ds(PAD, cy)
    x_has = (me > 0, me < n_gx - 1)
    y_has = (my > 0, my < n_gy - 1)
    both_sides = [(sx, sy) for sx in range(2) for sy in range(2)]

    def x_at(side):
        return me - 1 if side == 0 else me + 1

    def y_at(side):
        return my - 1 if side == 0 else my + 1

    barrier = pltpu.get_barrier_semaphore()

    def greet(k, carry):
        pl.semaphore_signal(barrier, inc=1, device_id=(lax.rem(me + k, n_gx), my), device_id_type=MESH)
        return carry

    lax.fori_loop(1, n_gx, greet, 0)
    beside_y = [(y_has[sy], (me, y_at(sy))) for sy in range(2)]
    beside_y += [(jnp.logical_and(x_has[sx], y_has[sy]), (x_at(sx), y_at(sy))) for sx, sy in both_sides]
    arrivals = n_gx - 1
    for there, device in beside_y:
        arrivals = arrivals + jnp.where(there, 1, 0)

        @pl.when(there)
        def _():
            pl.semaphore_signal(barrier, inc=1, device_id=device, device_id_type=MESH)

    load = pltpu.make_async_copy(noise, e0.at[pl.ds(2, cx), own, :], load_sem)
    load.start()
    small = [
        pltpu.make_async_copy(src, dst, small_sem.at[i])
        for i, (src, dst) in enumerate((
            (rate_in, rate), (coupling_in, coupling), (vertical_in, vertical),
            (slots_in, slots), (columns_in, columns), (coeffs_in, coeffs)))
    ]
    for copy in small:
        copy.start()

    for side in range(2):
        @pl.when(jnp.logical_not(x_has[side]))
        def _():
            for field in (e0, e2):
                for i in (0, 1) if side == 0 else (cx + 2, cx + 3):
                    field[i] = jnp.zeros(field.shape[1:], F32)
            beside_coef[1 - side] = jnp.zeros(beside_coef.shape[1:], F32)

        @pl.when(jnp.logical_not(y_has[side]))
        def _():
            for field in (e0, e2):
                for i in (1, cx + 2):
                    block = pl.ds(PAD - 8 if side == 0 else PAD + cy, 8)
                    field[i, block, :] = jnp.zeros((8, width), F32)
            for r in range(2):
                y_in[r, side] = jnp.zeros(y_in.shape[2:], F32)
            beside_coef[3 - side] = jnp.zeros(beside_coef.shape[1:], F32)

    pl.semaphore_wait(barrier, arrivals)

    def x_copy(r, side):
        field = fields[2 * r]
        row = 0 if side == 0 else cx - 2
        src = noise.at[pl.ds(row, 2)] if r == 0 else field.at[pl.ds(row + 2, 2), own, :]
        return pltpu.make_async_remote_copy(
            src_ref=src, dst_ref=field.at[pl.ds(cx + 2 if side == 0 else 0, 2), own, :],
            send_sem=xs_sem.at[r, side], recv_sem=xr_sem.at[r, side],
            device_id=(x_at(side), my), device_id_type=MESH)

    def y_copy(r, side):
        return pltpu.make_async_remote_copy(
            src_ref=y_out.at[r, side], dst_ref=y_in.at[r, 1 - side],
            send_sem=ys_sem.at[r, side], recv_sem=yr_sem.at[r, side],
            device_id=(me, y_at(side)), device_id_type=MESH)

    def corner_copy(r, sx, sy):
        field = fields[2 * r]
        row = 0 if sx == 0 else cx - 1
        col = 0 if sy == 0 else cy - 8
        src = noise.at[row, pl.ds(col, 8), :] if r == 0 else field.at[row + 2, pl.ds(PAD + col, 8), :]
        return pltpu.make_async_remote_copy(
            src_ref=src, dst_ref=field.at[cx + 2 if sx == 0 else 1, pl.ds(PAD + cy if sy == 0 else PAD - 8, 8), :],
            send_sem=cs_sem.at[r, 2 * sx + sy], recv_sem=cr_sem.at[r, 2 * sx + sy],
            device_id=(x_at(sx), y_at(sy)), device_id_type=MESH)

    def coef_copy(toward, part):
        return pltpu.make_async_remote_copy(
            src_ref=(rate_in, coupling_in)[part], dst_ref=beside_coef.at[toward, part],
            send_sem=ks_sem.at[toward, part], recv_sem=kr_sem.at[toward, part],
            device_id=(x_at(toward), my) if toward < 2 else (me, y_at(toward - 2)), device_id_type=MESH)

    def coef_has(toward):
        return x_has[toward] if toward < 2 else y_has[toward - 2]

    def coef_from(toward):
        return x_has[1 - toward] if toward < 2 else y_has[3 - toward]

    def send_rest(r):
        for side in range(2):
            @pl.when(x_has[side])
            def _():
                x_copy(r, side).start()
        for sx, sy in both_sides:
            @pl.when(jnp.logical_and(x_has[sx], y_has[sy]))
            def _():
                corner_copy(r, sx, sy).start()

    def send_y(r):
        field = fields[2 * r]
        for i in range(cx):
            y_out[r, 0, 2 * i:2 * i + 2, :] = field[i + 2, PAD:PAD + 2, :]
            y_out[r, 1, 2 * i:2 * i + 2, :] = field[i + 2, PAD + cy - 2:PAD + cy, :]
        for side in range(2):
            @pl.when(y_has[side])
            def _():
                y_copy(r, side).start()

    def receive(r):
        field = fields[2 * r]
        for side in range(2):
            @pl.when(y_has[1 - side])
            def _():
                y_copy(r, side).wait_recv()
        for i in range(cx):
            field[i + 2, PAD - 2:PAD, :] = y_in[r, 0, 2 * i:2 * i + 2, :]
            field[i + 2, PAD + cy:PAD + cy + 2, :] = y_in[r, 1, 2 * i:2 * i + 2, :]
        for side in range(2):
            @pl.when(x_has[1 - side])
            def _():
                x_copy(r, side).wait_recv()
        for sx, sy in both_sides:
            @pl.when(jnp.logical_and(x_has[1 - sx], y_has[1 - sy]))
            def _():
                corner_copy(r, sx, sy).wait_recv()

    def sent(r):
        for side in range(2):
            @pl.when(x_has[side])
            def _():
                x_copy(r, side).wait_send()

            @pl.when(y_has[side])
            def _():
                y_copy(r, side).wait_send()
        for sx, sy in both_sides:
            @pl.when(jnp.logical_and(x_has[sx], y_has[sy]))
            def _():
                corner_copy(r, sx, sy).wait_send()

    send_rest(0)
    load.wait()
    send_y(0)
    for toward in range(4):
        @pl.when(coef_has(toward))
        def _():
            for part in range(2):
                coef_copy(toward, part).start()
    for copy in small:
        copy.wait()

    q0 = coeffs[0] - coeffs[2]
    q1 = coeffs[1] - 3.0 * coeffs[3]
    q2 = 2.0 * coeffs[2]
    q3 = 4.0 * coeffs[3]

    def columns_hit(rows, first):
        return iota((rows, cy), 0) + first == iota((rows, cy), 1)

    def spread(src, dst, i, rows, hit):
        count = hit.shape[0]
        col = jnp.sum(jnp.where(hit, jnp.broadcast_to(src, (count, cy)), 0.0), axis=1, keepdims=True)
        dst[i, rows, :] = jnp.broadcast_to(col, (count, LANES))

    def spread_own():
        def row(i, carry):
            for src, dst in ((rate, rate_b), (coupling, coup_b)):
                spread(src[pl.ds(i, 1), :], dst, i + 1, pl.ds(8, cy), columns_hit(cy, 0))
            return carry

        lax.fori_loop(0, cx, row, 0)

    def spread_beside():
        for part, dst in enumerate((rate_b, coup_b)):
            spread(beside_coef[1, part, cx - 1:cx, :], dst, 0, pl.ds(8, cy), columns_hit(cy, 0))
            spread(beside_coef[0, part, 0:1, :], dst, cx + 1, pl.ds(8, cy), columns_hit(cy, 0))

        def row(i, carry):
            for part, dst in enumerate((rate_b, coup_b)):
                spread(beside_coef[3, part, pl.ds(i, 1), :], dst, i + 1, pl.ds(0, 8), columns_hit(8, cy - 8))
                spread(beside_coef[2, part, pl.ds(i, 1), :], dst, i + 1, pl.ds(8 + cy, 8), columns_hit(8, 0))
            return carry

        lax.fori_loop(0, cx, row, 0)

    def lateral(r, i, low, high):
        old, new = fields[r], fields[r + 1]
        rows = pl.ds(PAD + low, high - low)
        beside = (old[i + 1, rows, :] + old[i + 3, rows, :]) + (
            old[i + 2, PAD - 1 + low:PAD - 1 + high, :] + old[i + 2, PAD + 1 + low:PAD + 1 + high, :])
        a = rate_b[i + 1, 8 + low:8 + high, :]
        b = coup_b[i + 1, 8 + low:8 + high, :]
        if r == 2:
            a, b = q3 * a, q3 * b
        a = jnp.concatenate([a] * reps, axis=1)
        b = jnp.concatenate([b] * reps, axis=1)
        out = a * old[i + 2, rows, :] - b * beside
        if r == 2:
            out = out + total[i + 1, 8 + low:8 + high, :]
        new[i + 2, rows, :] = out

    def inner(r, edge):
        def row(i, carry):
            lateral(r, i, 8, cy - 8)
            return carry

        lax.fori_loop(edge, cx - edge, row, 0)

    def rim(r):
        lateral(r, -1, 0, cy)
        lateral(r, cx, 0, cy)
        lateral(r, 0, -8, cy + 8)
        lateral(r, cx - 1, -8, cy + 8)

        def row(i, carry):
            lateral(r, i, -8, 8)
            lateral(r, i, cy - 8, cy + 8)
            return carry

        lax.fori_loop(1, cx - 1, row, 0)

    def rim_two(r):
        for i in (0, 1, cx - 2, cx - 1):
            lateral(r, i, 0, cy)

        def row(i, carry):
            lateral(r, i, 0, 8)
            lateral(r, i, cy - 8, cy)
            return carry

        lax.fori_loop(2, cx - 2, row, 0)

    def make_weights():
        pick = (iota((LANES, depth), 0) % depth == iota((LANES, depth), 1)).astype(F32)
        tiled = dot_t(dot_t(pick, vertical[...]), pick)
        same = iota((LANES, LANES), 0) // depth == iota((LANES, LANES), 1) // depth
        eye = jnp.where(iota((LANES, LANES), 0) == iota((LANES, LANES), 1), 1.0, 0.0)
        v1 = jnp.where(same, tiled, 0.0)
        v2 = dot(v1, v1)
        v3 = dot(v1, v2)
        polys = (
            q0 * eye + q1 * v1 + q2 * v2 + q3 * v3,
            q1 * eye + (2.0 * q2) * v1 + (3.0 * q3) * v2,
            q2 * eye + (3.0 * q3) * v1,
        )
        for k, poly in enumerate(polys):
            high, low = split2(poly)
            for row in (0, LANES):
                weights[k, row:row + LANES, 0:LANES] = high
                weights[k, row:row + LANES, LANES:2 * LANES] = low

    def depth_block(ks, i, count, low, high):
        cells = count * (high - low)
        for t in range(reps):
            lanes = slice(t * LANES, (t + 1) * LANES)
            out = None
            for k in ks:
                value = fields[k][pl.ds(i + 2, count), PAD + low:PAD + high, lanes].reshape(cells, LANES)
                both = jnp.concatenate(split2(value), axis=1)
                one = jnp.dot(both, weights[k], preferred_element_type=F32)
                out = one if out is None else out + one
            out = (out[:, 0:LANES] + out[:, LANES:2 * LANES]).reshape(count, high - low, LANES)
            spot = (pl.ds(i + 1, count), slice(8 + low, 8 + high), lanes)
            total[spot] = out if 0 in ks else total[spot] + out

    def depth_own(ks):
        def part(g, carry):
            depth_block(ks, g * GROUP, GROUP, 0, cy)
            return carry

        lax.fori_loop(0, cx // GROUP, part, 0)

    def depth_beside(ks):
        depth_block(ks, -1, 1, 0, cy)
        depth_block(ks, cx, 1, 0, cy)
        depth_block(ks, 0, cx, -8, 0)
        depth_block(ks, 0, cx, cy, cy + 8)

    hit = iota((sensors, sensors), 0) == jnp.broadcast_to(slots[...], (sensors, sensors))
    cell = jnp.sum(jnp.where(hit, jnp.broadcast_to(columns[...], (sensors, sensors)), 0), axis=1, keepdims=True)
    spots_v[...] = jnp.broadcast_to(cell, (sensors, LANES))
    to_scalars = pltpu.make_async_copy(spots_v, spots, spot_sem)
    to_scalars.start()

    spread_own()
    inner(0, 1)
    make_weights()
    for toward in range(4):
        @pl.when(coef_from(toward))
        def _():
            for part in range(2):
                coef_copy(toward, part).wait_recv()
    spread_beside()
    receive(0)
    rim(0)
    rim_two(1)
    send_rest(1)
    send_y(1)
    inner(1, 2)
    depth_own((0, 1))
    depth_own((2,))
    depth_beside((0, 1))
    inner(2, 1)
    receive(1)
    depth_beside((2,))
    rim(2)
    store = pltpu.make_async_copy(e3.at[pl.ds(2, cx), own, :], sample, store_sem)
    store.start()
    to_scalars.wait()

    def center(k, carry):
        place = spots[k, 0]
        g_c[pl.ds(k, 1), :] = e3[place // cy + 2, pl.ds(place % cy + PAD, 1), :]
        return carry

    lax.fori_loop(0, sensors, center, 0, unroll=8)
    value = g_c[...]
    mean = value[:, 0:LANES]
    for t in range(1, reps):
        mean = mean + value[:, t * LANES:(t + 1) * LANES]
    mean = (mean + pltpu.roll(mean, depth, axis=1)) * (depth / width)
    g_c[...] = (value - jnp.concatenate([mean] * reps, axis=1)) * 0.5

    parts = ready.shape[0] // sensors
    per = ready.shape[0] // n_gx
    mine = pl.ds(pl.multiple_of(me * per, per), per)

    def peer_of(i):
        far = (i + 1) // 2
        return lax.rem(me + jnp.where(i % 2 == 1, far, n_gx - far), n_gx)

    def to_peer(i):
        peer = peer_of(i)
        return pltpu.make_async_remote_copy(
            src_ref=ready.at[pl.ds(pl.multiple_of(peer * per, per), per), :], dst_ref=grads.at[mine, :],
            send_sem=as_sem.at[i], recv_sem=ar_sem.at[i], device_id=(peer, my), device_id_type=MESH)

    def blocks_for(peer):
        for m in range(sensors // n_gx):
            k = peer * (sensors // n_gx) + m
            place = spots[k, 0]
            i = place // cy
            j = place % cy + PAD
            weight = g_c[pl.ds(k, 1), :]
            along_x = weight * (e3[i + 3, pl.ds(j, 1), :] - e3[i + 1, pl.ds(j, 1), :])
            along_y = weight * (e3[i + 2, pl.ds(j + 1, 1), :] - e3[i + 2, pl.ds(j - 1, 1), :])
            for d, product in enumerate((along_x, along_y)):
                for t in range(reps):
                    ready[pl.ds(k * parts + d * reps + t, 1), :] = product[:, t * LANES:(t + 1) * LANES]

    def start(s, carry):
        i = n_gx - 1 - s
        blocks_for(peer_of(i))
        to_peer(i).start()
        return carry

    lax.fori_loop(0, n_gx - 1, start, 0)
    blocks_for(me)
    keep = pltpu.make_async_copy(ready.at[mine, :], grads.at[mine, :], own_sem)
    keep.start()
    for r in range(2):
        sent(r)
    for toward in range(4):
        @pl.when(coef_has(toward))
        def _():
            for part in range(2):
                coef_copy(toward, part).wait_send()
    store.wait()
    keep.wait()

    def finish(i, carry):
        copy = to_peer(i)
        copy.wait_send()
        copy.wait_recv()
        return carry

    lax.fori_loop(1, n_gx, finish, 0)


def finish_kernel(sample_in, grads_in, sample, grads, flat, rows, in_sem, out_sem, load_sem, store_sem, whole):
    sensors, parts = rows.shape[0], rows.shape[1] // LANES
    first = pltpu.make_async_copy(grads_in, flat, in_sem)
    first.start()
    cut = sample.shape[0] // 4
    spots = [pl.ds(p * cut, cut) for p in range(4)]
    loads = [pltpu.make_async_copy(sample_in.at[s], whole.at[s], load_sem.at[p]) for p, s in enumerate(spots)]
    stores = [pltpu.make_async_copy(whole.at[s], sample.at[s], store_sem.at[p]) for p, s in enumerate(spots)]
    for copy in loads:
        copy.start()
    first.wait()
    for t in range(parts):
        rows[:, t * LANES:(t + 1) * LANES] = flat[pl.ds(t, sensors, stride=parts), :]
    last = pltpu.make_async_copy(rows, grads, out_sem)
    last.start()
    for load, store in zip(loads, stores):
        load.wait()
        store.start()
    for store in stores:
        store.wait()
    last.wait()


def shards(n_gx, n_gy, noise, rate, coupling, vertical, coeffs, columns, slots):
    cx, cy, width = noise.shape
    sensors = slots.shape[1]
    parts = 2 * width // LANES
    hbm = pl.BlockSpec(memory_space=pltpu.HBM)
    field = pltpu.VMEM((cx + 4, cy + 2 * PAD, width), F32)
    coef = pltpu.VMEM((cx + 2, cy + 16, LANES), F32)
    dma = pltpu.SemaphoreType.DMA
    sample, grads = pl.pallas_call(
        functools.partial(kernel, n_gx, n_gy),
        out_shape=(jax.ShapeDtypeStruct(noise.shape, F32),
                   jax.ShapeDtypeStruct((sensors * parts, LANES), F32)),
        in_specs=[hbm] * 7,
        out_specs=(hbm, hbm),
        scratch_shapes=[
            pltpu.VMEM(rate.shape, F32), pltpu.VMEM(coupling.shape, F32), pltpu.VMEM(vertical.shape, F32),
            pltpu.VMEM(slots.shape, jnp.int32), pltpu.VMEM(columns.shape, jnp.int32), pltpu.SMEM(coeffs.shape, F32),
            field, field, field, field, pltpu.VMEM((cx + 2, cy + 16, width), F32),
            coef, coef,
            pltpu.VMEM((3, 2 * LANES, 2 * LANES), BF16),
            pltpu.VMEM((2, 2, 2 * cx, width), F32), pltpu.VMEM((2, 2, 2 * cx, width), F32),
            pltpu.VMEM((4, 2, cx, cy), F32),
            pltpu.VMEM((sensors, LANES), jnp.int32), pltpu.SMEM((sensors, LANES), jnp.int32),
            pltpu.VMEM((sensors, width), F32), pltpu.VMEM((sensors * parts, LANES), F32),
            dma((6,)), dma, dma((2, 2)), dma((2, 2)), dma((2, 2)), dma((2, 2)),
            dma((2, 4)), dma((2, 4)), dma((4, 2)), dma((4, 2)),
            dma((n_gx,)), dma((n_gx,)), dma, dma, dma,
        ],
        compiler_params=pltpu.CompilerParams(
            collective_id=0, has_side_effects=True, vmem_limit_bytes=61 << 20),
    )(noise, rate, coupling, vertical, slots, columns, coeffs)
    return pl.pallas_call(
        finish_kernel,
        out_shape=(jax.ShapeDtypeStruct(noise.shape, F32),
                   jax.ShapeDtypeStruct((sensors, parts * LANES), F32)),
        in_specs=[pl.BlockSpec(memory_space=pl.ANY)] * 2,
        out_specs=(hbm, hbm),
        scratch_shapes=[
            pltpu.VMEM((sensors * parts, LANES), F32), pltpu.VMEM((sensors, parts * LANES), F32),
            dma, dma, dma((4,)), dma((4,)), pltpu.VMEM(noise.shape, F32),
        ],
        compiler_params=pltpu.CompilerParams(vmem_limit_bytes=61 << 20),
    )(sample, grads)


def solution(mesh):
    placed = (
        P("gx", "gy", None),
        P("gx", "gy"),
        P("gx", "gy"),
        P(),
        P(),
        P(("gx", "gy"), None),
        P(("gx", "gy"), None),
    )
    return jax.shard_map(
        functools.partial(shards, mesh.shape["gx"], mesh.shape["gy"]),
        mesh=mesh,
        in_specs=placed,
        out_specs=(P("gx", "gy", None), P(("gx", "gy"), None)),
        check_vma=False,
    )
```

time: 52.2 us -> 44.2 us (0.85)
  the two profiles are of different devices: /device:TPU:7 before, /device:TPU:4 now
where the time goes in v2:
time: 44.2 us; the launch traced here: 44 us
  Pallas kernels  43.4 us (98%)
  between operations  0.64 us (1%)
    pallas_call x1, Pallas kernels, shards(): pl.pallas_call(functools.partial(kernel, n_gx, n_gy), out_shape=(jax.Shap...  40.5 us
    pallas_call x1, Pallas kernels, shards(): pl.pallas_call(finish_kernel, out_shape=(jax.ShapeDtypeStruct(noise.shape...  2.96 us

profile of v2, /device:TPU:4, one launch (start us, length us, event | category | flops | bytes accessed | tf_op | source)
XLA Modules:
  0.0 44.0 jit_solution(18424727913150343541)
XLA Ops:
  0.6 40.5 %shard_map.86 = (f32[16,64,512]{2,1,0:T(8,128)}, f32[512,128]{1,0:T(8,128)}) custom-call(f32[16,64,512]{2,1,0:T(8,128)} %noise.1, f32[16,64]{1,0:T(8,128)} %rate_in.1, f32[16,64]{1,0:T(8,128)} %coupling_in.1, f32[64,64]{1,0:T(8,128)} %vertical_in.1, s32[1,64]{1,0:T(1,128)} %slots_in.1, s32[1,64]{1,0:T(1,128)} %columns_in.1, f32[4]{0:T(128)} %coeffs_in.1), custom_call_target="tpu_custom_call" | custom-call | tf_op jit(solution)/shard_map/pallas_call | solution.py:465
  41.1 3.0 %shard_map.87 = (f32[16,64,512]{2,1,0:T(8,128)}, f32[64,1024]{1,0:T(8,128)}) custom-call(f32[16,64,512]{2,1,0:T(8,128)} %get-tuple-element.4.sample_in, f32[512,128]{1,0:T(8,128)} %get-tuple-element.5.grads_in), custom_call_target="tpu_custom_call" | custom-call | tf_op jit(solution)/shard_map/pallas_call | solution.py:488

commit v3 on v2

--- a/solution.py
+++ b/solution.py
@@ -13,6 +13,7 @@
 BF16 = jnp.bfloat16
 LANES = 128
 GROUP = 4
+BATCH = 4
 PAD = 16
 
 
@@ -55,13 +56,12 @@
     def y_at(side):
         return my - 1 if side == 0 else my + 1
 
+    def peer_of(i):
+        far = (i + 1) // 2
+        return lax.rem(me + jnp.where(i % 2 == 1, far, n_gx - far), n_gx)
+
     barrier = pltpu.get_barrier_semaphore()
 
-    def greet(k, carry):
-        pl.semaphore_signal(barrier, inc=1, device_id=(lax.rem(me + k, n_gx), my), device_id_type=MESH)
-        return carry
-
-    lax.fori_loop(1, n_gx, greet, 0)
     beside_y = [(y_has[sy], (me, y_at(sy))) for sy in range(2)]
     beside_y += [(jnp.logical_and(x_has[sx], y_has[sy]), (x_at(sx), y_at(sy))) for sx, sy in both_sides]
     arrivals = n_gx - 1
@@ -72,8 +72,17 @@
         def _():
             pl.semaphore_signal(barrier, inc=1, device_id=device, device_id_type=MESH)
 
-    load = pltpu.make_async_copy(noise, e0.at[pl.ds(2, cx), own, :], load_sem)
-    load.start()
+    def greet(s, carry):
+        pl.semaphore_signal(barrier, inc=1, device_id=(peer_of(n_gx - 1 - s), my), device_id_type=MESH)
+        return carry
+
+    lax.fori_loop(0, n_gx - 1, greet, 0)
+    loads = [
+        pltpu.make_async_copy(noise.at[:, pl.ds(low, count), :], e0.at[pl.ds(2, cx), pl.ds(PAD + low, count), :], load_sem.at[i])
+        for i, (low, count) in enumerate(((0, 8), (cy - 8, 8), (8, cy - 16)))
+    ]
+    for copy in loads:
+        copy.start()
     small = [
         pltpu.make_async_copy(src, dst, small_sem.at[i])
         for i, (src, dst) in enumerate((
@@ -193,7 +202,8 @@
                 corner_copy(r, sx, sy).wait_send()
 
     send_rest(0)
-    load.wait()
+    loads[0].wait()
+    loads[1].wait()
     send_y(0)
     for toward in range(4):
         @pl.when(coef_has(toward))
@@ -202,6 +212,7 @@
                 coef_copy(toward, part).start()
     for copy in small:
         copy.wait()
+    loads[2].wait()
 
     q0 = coeffs[0] - coeffs[2]
     q1 = coeffs[1] - 3.0 * coeffs[3]
@@ -339,6 +350,7 @@
     spread_own()
     inner(0, 1)
     make_weights()
+    depth_own((0,))
     for toward in range(4):
         @pl.when(coef_from(toward))
         def _():
@@ -351,7 +363,7 @@
     send_rest(1)
     send_y(1)
     inner(1, 2)
-    depth_own((0, 1))
+    depth_own((1,))
     depth_own((2,))
     depth_beside((0, 1))
     inner(2, 1)
@@ -378,10 +390,6 @@
     parts = ready.shape[0] // sensors
     per = ready.shape[0] // n_gx
     mine = pl.ds(pl.multiple_of(me * per, per), per)
-
-    def peer_of(i):
-        far = (i + 1) // 2
-        return lax.rem(me + jnp.where(i % 2 == 1, far, n_gx - far), n_gx)
 
     def to_peer(i):
         peer = peer_of(i)
@@ -402,14 +410,21 @@
                 for t in range(reps):
                     ready[pl.ds(k * parts + d * reps + t, 1), :] = product[:, t * LANES:(t + 1) * LANES]
 
-    def start(s, carry):
-        i = n_gx - 1 - s
+    batch = BATCH if n_gx % BATCH == 0 else 1
+
+    def start(g, carry):
+        turns = [1 + g * batch + b for b in range(batch)]
+        for i in turns:
+            blocks_for(peer_of(i))
+        for i in turns:
+            to_peer(i).start()
+        return carry
+
+    lax.fori_loop(0, n_gx // batch - 1, start, 0)
+    for i in list(range(n_gx - batch + 1, n_gx)) + [0]:
         blocks_for(peer_of(i))
+    for i in range(n_gx - batch + 1, n_gx):
         to_peer(i).start()
-        return carry
-
-    lax.fori_loop(0, n_gx - 1, start, 0)
-    blocks_for(me)
     keep = pltpu.make_async_copy(ready.at[mine, :], grads.at[mine, :], own_sem)
     keep.start()
     for r in range(2):
@@ -431,24 +446,17 @@
     lax.fori_loop(1, n_gx, finish, 0)
 
 
-def finish_kernel(sample_in, grads_in, sample, grads, flat, rows, in_sem, out_sem, load_sem, store_sem, whole):
+def finish_kernel(sample_in, grads_in, sample, grads, rows, out_sem, store_sem):
     sensors, parts = rows.shape[0], rows.shape[1] // LANES
-    first = pltpu.make_async_copy(grads_in, flat, in_sem)
-    first.start()
     cut = sample.shape[0] // 4
     spots = [pl.ds(p * cut, cut) for p in range(4)]
-    loads = [pltpu.make_async_copy(sample_in.at[s], whole.at[s], load_sem.at[p]) for p, s in enumerate(spots)]
-    stores = [pltpu.make_async_copy(whole.at[s], sample.at[s], store_sem.at[p]) for p, s in enumerate(spots)]
-    for copy in loads:
+    stores = [pltpu.make_async_copy(sample_in.at[s], sample.at[s], store_sem.at[p]) for p, s in enumerate(spots)]
+    for copy in stores:
         copy.start()
-    first.wait()
     for t in range(parts):
-        rows[:, t * LANES:(t + 1) * LANES] = flat[pl.ds(t, sensors, stride=parts), :]
+        rows[:, t * LANES:(t + 1) * LANES] = grads_in[pl.ds(t, sensors, stride=parts), :]
     last = pltpu.make_async_copy(rows, grads, out_sem)
     last.start()
-    for load, store in zip(loads, stores):
-        load.wait()
-        store.start()
     for store in stores:
         store.wait()
     last.wait()
@@ -459,15 +467,15 @@
     sensors = slots.shape[1]
     parts = 2 * width // LANES
     hbm = pl.BlockSpec(memory_space=pltpu.HBM)
+    vmem = pl.BlockSpec(memory_space=pltpu.VMEM)
     field = pltpu.VMEM((cx + 4, cy + 2 * PAD, width), F32)
     coef = pltpu.VMEM((cx + 2, cy + 16, LANES), F32)
     dma = pltpu.SemaphoreType.DMA
     sample, grads = pl.pallas_call(
         functools.partial(kernel, n_gx, n_gy),
-        out_shape=(jax.ShapeDtypeStruct(noise.shape, F32),
-                   jax.ShapeDtypeStruct((sensors * parts, LANES), F32)),
+        out_shape=(pltpu.VMEM(noise.shape, F32), pltpu.VMEM((sensors * parts, LANES), F32)),
         in_specs=[hbm] * 7,
-        out_specs=(hbm, hbm),
+        out_specs=(vmem, vmem),
         scratch_shapes=[
             pltpu.VMEM(rate.shape, F32), pltpu.VMEM(coupling.shape, F32), pltpu.VMEM(vertical.shape, F32),
             pltpu.VMEM(slots.shape, jnp.int32), pltpu.VMEM(columns.shape, jnp.int32), pltpu.SMEM(coeffs.shape, F32),
@@ -478,24 +486,24 @@
             pltpu.VMEM((4, 2, cx, cy), F32),
             pltpu.VMEM((sensors, LANES), jnp.int32), pltpu.SMEM((sensors, LANES), jnp.int32),
             pltpu.VMEM((sensors, width), F32), pltpu.VMEM((sensors * parts, LANES), F32),
-            dma((6,)), dma, dma((2, 2)), dma((2, 2)), dma((2, 2)), dma((2, 2)),
+            dma((6,)), dma((3,)), dma((2, 2)), dma((2, 2)), dma((2, 2)), dma((2, 2)),
             dma((2, 4)), dma((2, 4)), dma((4, 2)), dma((4, 2)),
             dma((n_gx,)), dma((n_gx,)), dma, dma, dma,
         ],
         compiler_params=pltpu.CompilerParams(
-            collective_id=0, has_side_effects=True, vmem_limit_bytes=61 << 20),
-    )(noise, rate, coupling, vertical, slots, columns, coeffs)
+            collective_id=0, has_side_effects=True, vmem_limit_bytes=56 << 20),
+    )(*(pltpu.with_memory_space_constraint(arg, pltpu.HBM)
+        for arg in (noise, rate, coupling, vertical, slots, columns, coeffs)))
     return pl.pallas_call(
         finish_kernel,
         out_shape=(jax.ShapeDtypeStruct(noise.shape, F32),
                    jax.ShapeDtypeStruct((sensors, parts * LANES), F32)),
-        in_specs=[pl.BlockSpec(memory_space=pl.ANY)] * 2,
+        in_specs=[pl.BlockSpec(memory_space=pltpu.VMEM)] * 2,
         out_specs=(hbm, hbm),
         scratch_shapes=[
-            pltpu.VMEM((sensors * parts, LANES), F32), pltpu.VMEM((sensors, parts * LANES), F32),
-            dma, dma, dma((4,)), dma((4,)), pltpu.VMEM(noise.shape, F32),
+            pltpu.VMEM((sensors, parts * LANES), F32), dma, dma((4,)),
         ],
-        compiler_params=pltpu.CompilerParams(vmem_limit_bytes=61 << 20),
+        compiler_params=pltpu.CompilerParams(vmem_limit_bytes=16 << 20),
     )(sample, grads)
 
 

time: 44.2 us -> 41.8 us (0.946)
  the two profiles are of different devices: /device:TPU:4 before, /device:TPU:7 now
where the time goes in v3:
time: 41.8 us; the launch traced here: 41 us
  Pallas kernels  40.4 us (97%)
  between operations  0.64 us (2%)
    pallas_call x1, Pallas kernels, shards(): pl.pallas_call(functools.partial(kernel, n_gx, n_gy), out_shape=(pltpu.VM...  39 us
    pallas_call x1, Pallas kernels, shards(): pl.pallas_call(finish_kernel, out_shape=(jax.ShapeDtypeStruct(noise.shape...  1.44 us

profile of v3, /device:TPU:7, one launch (start us, length us, event | category | flops | bytes accessed | tf_op | source)
XLA Modules:
  0.0 41.0 jit_solution(6394900265138717639)
XLA Ops:
  0.6 39.0 %shard_map.86 = (f32[16,64,512]{2,1,0:T(8,128)S(1)}, f32[512,128]{1,0:T(8,128)S(1)}) custom-call(f32[16,64,512]{2,1,0:T(8,128)} %noise.1, f32[16,64]{1,0:T(8,128)} %rate_in.1, f32[16,64]{1,0:T(8,128)} %coupling_in.1, f32[64,64]{1,0:T(8,128)} %vertical_in.1, s32[1,64]{1,0:T(1,128)} %slots_in.1, s32[1,64]{1,0:T(1,128)} %columns_in.1, f32[4]{0:T(128)} %coeffs_in.1), custom_call_target="tpu_custom_call" | custom-call | tf_op jit(solution)/shard_map/pallas_call | solution.py:474
  39.6 1.4 %shard_map.87 = (f32[16,64,512]{2,1,0:T(8,128)}, f32[64,1024]{1,0:T(8,128)}) custom-call(f32[16,64,512]{2,1,0:T(8,128)S(1)} %get-tuple-element.4.sample_in, f32[512,128]{1,0:T(8,128)S(1)} %get-tuple-element.5.grads_in), custom_call_target="tpu_custom_call" | custom-call | tf_op jit(solution)/shard_map/pallas_call | solution.py:497

commit v4 on v3

--- a/solution.py
+++ b/solution.py
@@ -36,7 +36,7 @@
 
 def kernel(n_gx, n_gy, noise, rate_in, coupling_in, vertical_in, slots_in, columns_in, coeffs_in, sample, grads,
            rate, coupling, vertical, slots, columns, coeffs, e0, e1, e2, e3, total, rate_b, coup_b, weights,
-           y_out, y_in, beside_coef, spots_v, spots, g_c, ready,
+           y_out, y_in, beside_coef, spots_v, spots, ready,
            small_sem, load_sem, xs_sem, xr_sem, ys_sem, yr_sem, cs_sem, cr_sem, ks_sem, kr_sem, as_sem, ar_sem, store_sem, own_sem, spot_sem):
     cx, cy, width = noise.shape
     depth = vertical.shape[0]
@@ -149,15 +149,17 @@
     def coef_from(toward):
         return x_has[1 - toward] if toward < 2 else y_has[3 - toward]
 
-    def send_rest(r):
+    def send_corners(r):
+        for sx, sy in both_sides:
+            @pl.when(jnp.logical_and(x_has[sx], y_has[sy]))
+            def _():
+                corner_copy(r, sx, sy).start()
+
+    def send_x(r):
         for side in range(2):
             @pl.when(x_has[side])
             def _():
                 x_copy(r, side).start()
-        for sx, sy in both_sides:
-            @pl.when(jnp.logical_and(x_has[sx], y_has[sy]))
-            def _():
-                corner_copy(r, sx, sy).start()
 
     def send_y(r):
         field = fields[2 * r]
@@ -201,15 +203,16 @@
             def _():
                 corner_copy(r, sx, sy).wait_send()
 
-    send_rest(0)
-    loads[0].wait()
-    loads[1].wait()
-    send_y(0)
+    send_corners(0)
     for toward in range(4):
         @pl.when(coef_has(toward))
         def _():
             for part in range(2):
                 coef_copy(toward, part).start()
+    loads[0].wait()
+    loads[1].wait()
+    send_y(0)
+    send_x(0)
     for copy in small:
         copy.wait()
     loads[2].wait()
@@ -360,8 +363,9 @@
     receive(0)
     rim(0)
     rim_two(1)
-    send_rest(1)
+    send_corners(1)
     send_y(1)
+    send_x(1)
     inner(1, 2)
     depth_own((1,))
     depth_own((2,))
@@ -371,21 +375,7 @@
     depth_beside((2,))
     rim(2)
     store = pltpu.make_async_copy(e3.at[pl.ds(2, cx), own, :], sample, store_sem)
-    store.start()
     to_scalars.wait()
-
-    def center(k, carry):
-        place = spots[k, 0]
-        g_c[pl.ds(k, 1), :] = e3[place // cy + 2, pl.ds(place % cy + PAD, 1), :]
-        return carry
-
-    lax.fori_loop(0, sensors, center, 0, unroll=8)
-    value = g_c[...]
-    mean = value[:, 0:LANES]
-    for t in range(1, reps):
-        mean = mean + value[:, t * LANES:(t + 1) * LANES]
-    mean = (mean + pltpu.roll(mean, depth, axis=1)) * (depth / width)
-    g_c[...] = (value - jnp.concatenate([mean] * reps, axis=1)) * 0.5
 
     parts = ready.shape[0] // sensors
     per = ready.shape[0] // n_gx
@@ -403,7 +393,12 @@
             place = spots[k, 0]
             i = place // cy
             j = place % cy + PAD
-            weight = g_c[pl.ds(k, 1), :]
+            value = e3[i + 2, pl.ds(j, 1), :]
+            mean = value[:, 0:LANES]
+            for t in range(1, reps):
+                mean = mean + value[:, t * LANES:(t + 1) * LANES]
+            mean = (mean + pltpu.roll(mean, depth, axis=1)) * (depth / width)
+            weight = (value - jnp.concatenate([mean] * reps, axis=1)) * 0.5
             along_x = weight * (e3[i + 3, pl.ds(j, 1), :] - e3[i + 1, pl.ds(j, 1), :])
             along_y = weight * (e3[i + 2, pl.ds(j + 1, 1), :] - e3[i + 2, pl.ds(j - 1, 1), :])
             for d, product in enumerate((along_x, along_y)):
@@ -427,6 +422,7 @@
         to_peer(i).start()
     keep = pltpu.make_async_copy(ready.at[mine, :], grads.at[mine, :], own_sem)
     keep.start()
+    store.start()
     for r in range(2):
         sent(r)
     for toward in range(4):
@@ -485,7 +481,7 @@
             pltpu.VMEM((2, 2, 2 * cx, width), F32), pltpu.VMEM((2, 2, 2 * cx, width), F32),
             pltpu.VMEM((4, 2, cx, cy), F32),
             pltpu.VMEM((sensors, LANES), jnp.int32), pltpu.SMEM((sensors, LANES), jnp.int32),
-            pltpu.VMEM((sensors, width), F32), pltpu.VMEM((sensors * parts, LANES), F32),
+            pltpu.VMEM((sensors * parts, LANES), F32),
             dma((6,)), dma((3,)), dma((2, 2)), dma((2, 2)), dma((2, 2)), dma((2, 2)),
             dma((2, 4)), dma((2, 4)), dma((4, 2)), dma((4, 2)),
             dma((n_gx,)), dma((n_gx,)), dma, dma, dma,

time: 41.8 us -> 39.4 us (0.943); the launches traced: 41 us -> 39.2 us
  Pallas kernels: 40.4 us -> 38.6 us
    pallas_call x1, Pallas kernels: 39 us -> 37.1 us  [shards(): pl.pallas_call(functools.partial(kernel, n_gx, n_gy), out_shape=(pltpu.VM...]
where the time goes in v4:
time: 39.4 us; the launch traced here: 39.2 us
  Pallas kernels  38.6 us (98%)
  between operations  0.64 us (2%)
    pallas_call x1, Pallas kernels, shards(): pl.pallas_call(functools.partial(kernel, n_gx, n_gy), out_shape=(pltpu.VM...  37.1 us
    pallas_call x1, Pallas kernels, shards(): pl.pallas_call(finish_kernel, out_shape=(jax.ShapeDtypeStruct(noise.shape...  1.44 us

profile of v4, /device:TPU:7, one launch (start us, length us, event | category | flops | bytes accessed | tf_op | source)
XLA Modules:
  0.0 39.2 jit_solution(1377548714430870954)
XLA Ops:
  0.6 37.1 %shard_map.86 = (f32[16,64,512]{2,1,0:T(8,128)S(1)}, f32[512,128]{1,0:T(8,128)S(1)}) custom-call(f32[16,64,512]{2,1,0:T(8,128)} %noise.1, f32[16,64]{1,0:T(8,128)} %rate_in.1, f32[16,64]{1,0:T(8,128)} %coupling_in.1, f32[64,64]{1,0:T(8,128)} %vertical_in.1, s32[1,64]{1,0:T(1,128)} %slots_in.1, s32[1,64]{1,0:T(1,128)} %columns_in.1, f32[4]{0:T(128)} %coeffs_in.1), custom_call_target="tpu_custom_call" | custom-call | tf_op jit(solution)/shard_map/pallas_call | solution.py:470
  37.8 1.4 %shard_map.87 = (f32[16,64,512]{2,1,0:T(8,128)}, f32[64,1024]{1,0:T(8,128)}) custom-call(f32[16,64,512]{2,1,0:T(8,128)S(1)} %get-tuple-element.4.sample_in, f32[512,128]{1,0:T(8,128)S(1)} %get-tuple-element.5.grads_in), custom_call_target="tpu_custom_call" | custom-call | tf_op jit(solution)/shard_map/pallas_call | solution.py:493

commit v5 on v4

--- a/solution.py
+++ b/solution.py
@@ -287,10 +287,11 @@
 
         lax.fori_loop(1, cx - 1, row, 0)
 
-    def rim_two(r):
+    def rim_rows(r):
         for i in (0, 1, cx - 2, cx - 1):
             lateral(r, i, 0, cy)
 
+    def rim_columns(r):
         def row(i, carry):
             lateral(r, i, 0, 8)
             lateral(r, i, cy - 8, cy)
@@ -362,10 +363,11 @@
     spread_beside()
     receive(0)
     rim(0)
-    rim_two(1)
+    rim_rows(1)
     send_corners(1)
+    send_x(1)
+    rim_columns(1)
     send_y(1)
-    send_x(1)
     inner(1, 2)
     depth_own((1,))
     depth_own((2,))

time: 39.4 us -> 39.1 us (level)
  no operation moved by 1% of the time
where the time goes in v5:
time: 39.1 us; the launch traced here: 39 us
  Pallas kernels  38.3 us (98%)
  between operations  0.64 us (2%)
    pallas_call x1, Pallas kernels, shards(): pl.pallas_call(functools.partial(kernel, n_gx, n_gy), out_shape=(pltpu.VM...  36.9 us
    pallas_call x1, Pallas kernels, shards(): pl.pallas_call(finish_kernel, out_shape=(jax.ShapeDtypeStruct(noise.shape...  1.44 us

profile of v5, /device:TPU:7, one launch (start us, length us, event | category | flops | bytes accessed | tf_op | source)
XLA Modules:
  0.0 39.0 jit_solution(14264776634149939362)
XLA Ops:
  0.6 36.9 %shard_map.86 = (f32[16,64,512]{2,1,0:T(8,128)S(1)}, f32[512,128]{1,0:T(8,128)S(1)}) custom-call(f32[16,64,512]{2,1,0:T(8,128)} %noise.1, f32[16,64]{1,0:T(8,128)} %rate_in.1, f32[16,64]{1,0:T(8,128)} %coupling_in.1, f32[64,64]{1,0:T(8,128)} %vertical_in.1, s32[1,64]{1,0:T(1,128)} %slots_in.1, s32[1,64]{1,0:T(1,128)} %columns_in.1, f32[4]{0:T(128)} %coeffs_in.1), custom_call_target="tpu_custom_call" | custom-call | tf_op jit(solution)/shard_map/pallas_call | solution.py:472
  37.5 1.4 %shard_map.87 = (f32[16,64,512]{2,1,0:T(8,128)}, f32[64,1024]{1,0:T(8,128)}) custom-call(f32[16,64,512]{2,1,0:T(8,128)S(1)} %get-tuple-element.4.sample_in, f32[512,128]{1,0:T(8,128)S(1)} %get-tuple-element.5.grads_in), custom_call_target="tpu_custom_call" | custom-call | tf_op jit(solution)/shard_map/pallas_call | solution.py:495

commit v6 on v5

--- a/solution.py
+++ b/solution.py
@@ -171,7 +171,7 @@
             def _():
                 y_copy(r, side).start()
 
-    def receive(r):
+    def receive_y(r):
         field = fields[2 * r]
         for side in range(2):
             @pl.when(y_has[1 - side])
@@ -180,6 +180,8 @@
         for i in range(cx):
             field[i + 2, PAD - 2:PAD, :] = y_in[r, 0, 2 * i:2 * i + 2, :]
             field[i + 2, PAD + cy:PAD + cy + 2, :] = y_in[r, 1, 2 * i:2 * i + 2, :]
+
+    def receive_x(r):
         for side in range(2):
             @pl.when(x_has[1 - side])
             def _():
@@ -274,18 +276,19 @@
 
         lax.fori_loop(edge, cx - edge, row, 0)
 
-    def rim(r):
+    def rim_y(r):
+        def row(i, carry):
+            lateral(r, i, -8, 8)
+            lateral(r, i, cy - 8, cy + 8)
+            return carry
+
+        lax.fori_loop(1, cx - 1, row, 0)
+
+    def rim_x(r):
         lateral(r, -1, 0, cy)
         lateral(r, cx, 0, cy)
         lateral(r, 0, -8, cy + 8)
         lateral(r, cx - 1, -8, cy + 8)
-
-        def row(i, carry):
-            lateral(r, i, -8, 8)
-            lateral(r, i, cy - 8, cy + 8)
-            return carry
-
-        lax.fori_loop(1, cx - 1, row, 0)
 
     def rim_rows(r):
         for i in (0, 1, cx - 2, cx - 1):
@@ -339,9 +342,11 @@
 
         lax.fori_loop(0, cx // GROUP, part, 0)
 
-    def depth_beside(ks):
+    def depth_x(ks):
         depth_block(ks, -1, 1, 0, cy)
         depth_block(ks, cx, 1, 0, cy)
+
+    def depth_y(ks):
         depth_block(ks, 0, cx, -8, 0)
         depth_block(ks, 0, cx, cy, cy + 8)
 
@@ -361,8 +366,10 @@
             for part in range(2):
                 coef_copy(toward, part).wait_recv()
     spread_beside()
-    receive(0)
-    rim(0)
+    receive_y(0)
+    rim_y(0)
+    receive_x(0)
+    rim_x(0)
     rim_rows(1)
     send_corners(1)
     send_x(1)
@@ -371,11 +378,15 @@
     inner(1, 2)
     depth_own((1,))
     depth_own((2,))
-    depth_beside((0, 1))
+    depth_x((0, 1))
+    depth_y((0, 1))
     inner(2, 1)
-    receive(1)
-    depth_beside((2,))
-    rim(2)
+    receive_y(1)
+    depth_y((2,))
+    rim_y(2)
+    receive_x(1)
+    depth_x((2,))
+    rim_x(2)
     store = pltpu.make_async_copy(e3.at[pl.ds(2, cx), own, :], sample, store_sem)
     to_scalars.wait()
 

time: 39.1 us -> 39.3 us (level)
  no operation moved by 1% of the time
where the time goes in v6:
time: 39.3 us; the launch traced here: 39.1 us
  Pallas kernels  38.5 us (98%)
  between operations  0.64 us (2%)
    pallas_call x1, Pallas kernels, shards(): pl.pallas_call(functools.partial(kernel, n_gx, n_gy), out_shape=(pltpu.VM...  37.1 us
    pallas_call x1, Pallas kernels, shards(): pl.pallas_call(finish_kernel, out_shape=(jax.ShapeDtypeStruct(noise.shape...  1.44 us

profile of v6, /device:TPU:7, one launch (start us, length us, event | category | flops | bytes accessed | tf_op | source)
XLA Modules:
  0.0 39.1 jit_solution(7519727795775796938)
XLA Ops:
  0.6 37.1 %shard_map.86 = (f32[16,64,512]{2,1,0:T(8,128)S(1)}, f32[512,128]{1,0:T(8,128)S(1)}) custom-call(f32[16,64,512]{2,1,0:T(8,128)} %noise.1, f32[16,64]{1,0:T(8,128)} %rate_in.1, f32[16,64]{1,0:T(8,128)} %coupling_in.1, f32[64,64]{1,0:T(8,128)} %vertical_in.1, s32[1,64]{1,0:T(1,128)} %slots_in.1, s32[1,64]{1,0:T(1,128)} %columns_in.1, f32[4]{0:T(128)} %coeffs_in.1), custom_call_target="tpu_custom_call" | custom-call | tf_op jit(solution)/shard_map/pallas_call | solution.py:483
  37.7 1.4 %shard_map.87 = (f32[16,64,512]{2,1,0:T(8,128)}, f32[64,1024]{1,0:T(8,128)}) custom-call(f32[16,64,512]{2,1,0:T(8,128)S(1)} %get-tuple-element.4.sample_in, f32[512,128]{1,0:T(8,128)S(1)} %get-tuple-element.5.grads_in), custom_call_target="tpu_custom_call" | custom-call | tf_op jit(solution)/shard_map/pallas_call | solution.py:506
